TPU v7x, 1024 devices: a whole 4x8x16 slice. The times are simulated.
1024 devices in a mesh: dp: 32 (over y, x), fsdp: 32 (over z, core).
Axes of the slice: x: 4, y: 8, z: 16, core: 2. Of those that a mesh axis runs over, the one named last changes fastest.
Arguments:
- activations: bfloat16 [131072, 8192], P('dp', 'fsdp'), may hold values from -0.3984375 to 0.3984375
- out_grads: bfloat16 [131072, 1024], P('dp', 'fsdp'), may hold values from -0.3984375 to 0.3984375
- tile_domain: int32 [1024, 1], P('dp'), may hold values from 0 to 63
- adapter_a: bfloat16 [64, 16, 8192], P('dp', None, 'fsdp'), may hold values from -1.5 to 1.5
- adapter_b: bfloat16 [64, 16, 1024], P('dp', None, 'fsdp'), may hold values from -0.1875 to 0.1875
Outputs:
- grad_a: float32 [64, 16, 8192], P('dp', None, 'fsdp')
- grad_b: float32 [64, 16, 1024], P('dp', None, 'fsdp')
All inputs are finite; a program needn't handle non-finite values.
Results may differ from a plain program's by a relative error of at most 0.0029.
Values may be sent and summed in bfloat16 or wider, within the bound.
No kernel may reach another device: no remote copies, remote signals or barrier semaphores. Data moves between devices by JAX's collectives and lax.ppermute only.
A program may use at most 32 MiB of HBM per device.

v0:
```python
import jax
import jax.numpy as jnp
from jax import lax
from jax.sharding import PartitionSpec as P

TILE = 128


def shards(activations, out_grads, tile_domain, adapter_a, adapter_b):
    highest = lax.Precision.HIGHEST
    group_rows, feature_cols = activations.shape
    kv_cols = out_grads.shape[1]
    owned = adapter_a.shape[0]
    all_a, all_b = (
        lax.all_gather(adapter_a, "dp", axis=0, tiled=True),
        lax.all_gather(adapter_b, "dp", axis=0, tiled=True),
    )
    domain_count = all_a.shape[0]
    tile_ids = tile_domain[:, 0]
    tile_count = tile_ids.shape[0]
    act_tiles = activations.reshape(tile_count, TILE, feature_cols)
    grad_tiles = out_grads.reshape(tile_count, TILE, kv_cols)
    chosen_a = jnp.take(all_a, tile_ids, axis=0)
    chosen_b = jnp.take(all_b, tile_ids, axis=0)
    down_part = jnp.einsum("tkd,trd->tkr", act_tiles, chosen_a, preferred_element_type=jnp.float32)
    up_part = jnp.einsum("tkc,trc->tkr", grad_tiles, chosen_b, preferred_element_type=jnp.float32)
    down_full, up_full = lax.psum((down_part, up_part), "fsdp")
    down_rounded = down_full.astype(jnp.bfloat16)
    up_rounded = up_full.astype(jnp.bfloat16)
    domain_range = jnp.arange(domain_count, dtype=jnp.int32)[None, :]
    onehot_all = (tile_ids[:, None] == domain_range).astype(jnp.float32)
    a_terms = jnp.einsum("tkd,tkr->trd", act_tiles, up_rounded, preferred_element_type=jnp.float32)
    grad_a_part = 2.0 * jnp.einsum("te,trd->erd", onehot_all, a_terms, precision=highest)
    b_terms = jnp.einsum(
        "tkr,tkc->trc", down_rounded, grad_tiles, preferred_element_type=jnp.float32
    )
    grad_b_part = 2.0 * jnp.einsum("te,trc->erc", onehot_all, b_terms, precision=highest)
    total_a, total_b = lax.psum((grad_a_part, grad_b_part), "dp")
    first = lax.axis_index("dp") * owned
    grad_a = lax.dynamic_slice_in_dim(total_a, first, owned, 0)
    grad_b = lax.dynamic_slice_in_dim(total_b, first, owned, 0)
    return (grad_a, grad_b)


def solution(mesh):
    placed = (
        P("dp", "fsdp"),
        P("dp", "fsdp"),
        P("dp", None),
        P("dp", None, "fsdp"),
        P("dp", None, "fsdp"),
    )
    return jax.shard_map(
        shards,
        mesh=mesh,
        in_specs=placed,
        out_specs=(P("dp", None, "fsdp"), P("dp", None, "fsdp")),
        check_vma=False,
    )
```

profile of v0, /device:TPU:16, one launch (start us, length us, event | category | flops | bytes accessed | tf_op | source)
XLA Modules:
  0.0 406.1 jit_solution(16817626554921177704)
XLA Ops:
  7.2 0.0 copy-start
  7.2 0.0 copy-start.2
  7.2 0.0 all-reduce.5.cloned.1.call-start
  7.2 0.8 fusion.23
  8.0 0.7 and_bitcast_fusion
  8.7 0.0 copy-start.1
  8.7 57.3 %all_gather.7 = bf16[64,16,256]{2,1,0:T(8,128)(2,1)S(1)} all-gather(bf16[2,16,256]{2,1,0:T(8,128)(2,1)} %param.8), channel_id=1, replica_groups=mesh['dp'=32,'fsdp'=32] {'dp'}, dimensions={0}, use_global_device_ids=true | all-gather | bytes 540672 | tf_op jit(solution)/shard_map/all_gather | solution.py:15
  66.0 0.6 gather_fusion.1
  66.6 0.0 copy-done
  66.6 0.7 convolution_bitcast_fusion
  67.3 0.0 copy-done.2
  67.3 48.3 %all_gather.6 = bf16[64,16,32]{2,1,0:T(8,128)(2,1)S(1)} all-gather(bf16[2,16,32]{2,1,0:T(8,128)(2,1)S(1)} %copy-done.2), channel_id=1, replica_groups=mesh['dp'=32,'fsdp'=32] {'dp'}, dimensions={0}, use_global_device_ids=true | all-gather | bytes 67584 | tf_op jit(solution)/shard_map/all_gather | solution.py:16
  115.6 0.6 gather_fusion
  116.2 0.0 copy-done.1
  116.2 0.3 convolution_bitcast_fusion.1
  116.5 0.0 copy-start.3
  116.5 99.2 %all-reduce.6 = (bf16[32,128,16]{1,2,0:T(8,128)(2,1)S(1)}, bf16[32,128,16]{1,2,0:T(8,128)(2,1)S(1)}) all-reduce(f32[32,128,16]{1,2,0:T(8,128)S(1)} %convolution_bitcast_fusion.1, f32[32,128,16]{1,2,0:T(8,128)S(1)} %convolution_bitcast_fusion), channel_id=1, replica_groups=mesh['dp'=32,'fsdp'=32] {'fsdp'}, use_global_device_ids=true, to_apply=%region_0.1 | all-reduce | flops 131072 | bytes 786432 | tf_op jit(solution)/shard_map/psum | solution.py:27
  215.8 0.4 fusion.24
  216.2 0.2 fusion.1
  216.4 0.0 copy-done.3
  216.4 1.9 convolution_multiply_fusion
  218.4 1.3 convolution_multiply_fusion.1
  219.6 0.0 all-reduce.5.cloned.1.call-update
  219.7 176.5 %all-reduce.5.cloned.1.call-done = (f32[64,16,256]{2,0,1:T(8,128)}, f32[64,16,32]{2,0,1:T(8,128)}) async-done(((f32[64,16,256]{2,0,1:T(8,128)}, f32[64,16,32]{2,0,1:T(8,128)}), (f32[64,16,256]{2,0,1:T(8,128)}, f32[64,16,32]{2,0,1:T(8,128)})) %all-reduce.5.cloned.1.call-update) | async-done | bytes 1179664 | tf_op jit(solution)/shard_map/psum | solution.py:38
  396.2 0.9 constant_dynamic-slice_fusion.1
  397.1 0.6 copy.9
  397.8 0.8 constant_dynamic-slice_fusion
  398.6 0.6 copy.10
  (1 shorter events, 0.0 us)
Async XLA Ops:
  7.2 59.5 %copy-start = (bf16[4096,256]{1,0:T(8,128)(2,1)S(1)}, bf16[4096,256]{1,0:T(8,128)(2,1)}, u32[]{:S(2)}) copy-start(bf16[4096,256]{1,0:T(8,128)(2,1)} %param.5) | copy-start | bytes 6291460
  7.2 60.1 %copy-start.2 = (bf16[2,16,32]{2,1,0:T(8,128)(2,1)S(1)}, bf16[2,16,32]{2,1,0:T(8,128)(2,1)}, u32[]{:S(2)}) copy-start(bf16[2,16,32]{2,1,0:T(8,128)(2,1)} %param.9) | copy-start | bytes 6148
  7.2 389.0 %all-reduce.5.cloned.1.call-start = ((), (), s32[]{:S(2)}) async-start(), calls=%async_computation | async-start | bytes 3145728 | tf_op jit(solution)/shard_map/psum | solution.py:38
  8.7 107.5 %copy-start.1 = (bf16[4096,32]{0,1:T(8,128)(2,1)S(1)}, bf16[4096,32]{0,1:T(8,128)(2,1)}, u32[]{:S(2)}) copy-start(bf16[4096,32]{0,1:T(8,128)(2,1)} %param.6) | copy-start | bytes 786436
  116.5 99.9 %copy-start.3 = (s32[32,1]{0,1:T(1,128)S(1)}, s32[32,1]{0,1:T(1,128)}, u32[]{:S(2)}) copy-start(s32[32,1]{0,1:T(1,128)} %param.7) | copy-start | bytes 388
Sparse Core Ops, SparseCore 0:
  219.8 176.3 all-reduce.4
where the time goes:
time: 406 us
  blocking collectives  205 us (50%)
  waiting for transfers between devices  177 us (44%)
  between operations  14.1 us (3%)
  matrix products  4.82 us (1%)
  local copies, waits for them, and re-layouts  4.18 us (1%)
    psum x1, waiting for transfers between devices, shards(): total_a, total_b = lax.psum((grad_a_part, grad_b_part), 'dp')  177 us
    psum x1, blocking collectives, shards(): down_full, up_full = lax.psum((down_part, up_part), 'fsdp')  99.2 us
    all_gather x1, blocking collectives, shards(): lax.all_gather(adapter_a, 'dp', axis=0, tiled=True)  57.3 us
    all_gather x1, blocking collectives, shards(): lax.all_gather(adapter_b, 'dp', axis=0, tiled=True)  48.3 us
  transfers between devices with their start and end apart: 1, of which 1 were waited for; matrix products, arithmetic and copies ran while one was open for 0% of the time, Pallas kernels for 0%

commit v1 on v0

v1 whole, which is shorter than its diff:
```python
import jax
import jax.numpy as jnp
from jax import lax
from jax.experimental import pallas as pl
from jax.experimental.pallas import tpu as pltpu
from jax.sharding import PartitionSpec as P

F32 = jnp.float32
BF16 = jnp.bfloat16
TILE = 128
RANK = 16
OWNERS = 32
DEPTH = 16
ROWS = 72

NT = (((1,), (1,)), ((), ()))
NN = (((1,), (0,)), ((), ()))
PARAMS = pltpu.CompilerParams(vmem_limit_bytes=32 * 1024 * 1024)
VMEM = pl.BlockSpec(memory_space=pltpu.VMEM)
SMEM = pl.BlockSpec(memory_space=pltpu.SMEM)


def call(kernel, out, specs, *operands, scratch=()):
    return pl.pallas_call(
        kernel,
        out_shape=out,
        in_specs=specs,
        out_specs=jax.tree.map(lambda _: VMEM, out),
        scratch_shapes=scratch,
        compiler_params=PARAMS,
    )(*operands)


def lane_block():
    return lax.broadcasted_iota(jnp.int32, (8, 128), 1) // 32


def pack_kernel(a_ref, b_ref, out_ref):
    pieces = []
    for i in range(2):
        pieces += [a_ref[i, :, 0:128], a_ref[i, :, 128:256]]
    rows = lax.broadcasted_iota(jnp.int32, (32, 128), 0)
    lanes = lax.broadcasted_iota(jnp.int32, (32, 128), 1)
    small = jnp.zeros((8, 128), F32)
    for i in range(2):
        for h in range(2):
            place = jnp.where(lanes == rows + 32 * (2 * i + h), 1.0, 0.0).astype(BF16)
            spread = lax.dot_general(b_ref[i], place, NN, preferred_element_type=F32)
            small = small + spread[8 * h : 8 * h + 8]
    big = jnp.concatenate(pieces, axis=0)
    small = small.astype(BF16)
    for o in range(OWNERS):
        out_ref[o, 0:64] = big
        out_ref[o, 64:72] = small


def tile_og(og_ref, tile):
    og = og_ref[:, pl.ds(pl.multiple_of(tile * TILE, TILE), TILE)]
    return jnp.concatenate([og, og, og, og], axis=0)


def tile_act(act_ref, tile):
    return act_ref[pl.ds(pl.multiple_of(tile * TILE, TILE), TILE), :]


def partial_kernel(ids_ref, w_ref, act_ref, og_ref, keep_ref, send_ref):
    core = lax.axis_index("fsdp") % 2
    block = lane_block()
    for out_ref, parity in ((send_ref, 1 - core), (keep_ref, core)):
        for z in range(DEPTH):
            tile = 2 * z + parity
            e = ids_ref[tile]
            o = e // 2
            i = e % 2
            a = w_ref[o, pl.ds(pl.multiple_of(i * 32, 32), 32), :]
            b = w_ref[o, 64:72, :].astype(F32)
            left = jnp.concatenate([a[0:16], a[16:32]], axis=1)
            down = lax.dot_general(left, tile_act(act_ref, tile), NT, preferred_element_type=F32)
            spread = jnp.concatenate(
                [jnp.where(block == 2 * i, b, 0.0), jnp.where(block == 2 * i + 1, b, 0.0)], axis=0
            ).astype(BF16)
            up = lax.dot_general(spread, tile_og(og_ref, tile), NN, preferred_element_type=F32)
            out_ref[z, 0:16] = down
            out_ref[z, 16:32] = up


def round_kernel(in_ref, out_ref):
    total = in_ref[0]
    for z in range(1, DEPTH):
        total = total + in_ref[z]
    total = total.astype(BF16)
    for z in range(DEPTH):
        out_ref[z] = total


def grad_kernel(ids_ref, act_ref, og_ref, own_ref, other_ref, out_ref, acc_ref, ga_ref, gb_ref):
    core = lax.axis_index("fsdp") % 2
    acc_ref[...] = jnp.zeros_like(acc_ref)
    block = lane_block()
    for p, (in_ref, parity) in enumerate(((own_ref, core), (other_ref, 1 - core))):
        for z in range(DEPTH):
            tile = 2 * z + parity
            down = in_ref[z, 0:16]
            up = in_ref[z, 16:32]
            ga_ref[p * DEPTH + z] = lax.dot_general(up, tile_act(act_ref, tile), NN, preferred_element_type=F32)
            gb_ref[p * DEPTH + z] = lax.dot_general(down, tile_og(og_ref, tile), NT, preferred_element_type=F32)
    for p, parity in enumerate((core, 1 - core)):
        for z in range(DEPTH):
            e = ids_ref[2 * z + parity]
            o = e // 2
            i = e % 2
            ga = ga_ref[p * DEPTH + z]
            gb = gb_ref[p * DEPTH + z]
            at = pl.ds(pl.multiple_of(i * 32, 32), 32)
            acc_ref[o, at, :] += jnp.concatenate([ga[:, 0:128], ga[:, 128:256]], axis=0)
            acc_ref[o, 64:72, :] += jnp.where(block == 2 * i, gb[0:8], 0.0) + jnp.where(block == 2 * i + 1, gb[8:16], 0.0)
    for o in range(OWNERS):
        out_ref[o] = (2.0 * acc_ref[o]).astype(BF16)


def final_kernel(in_ref, ga_ref, gb_ref):
    total = in_ref[0].astype(F32)
    for o in range(1, OWNERS):
        total = total + in_ref[o].astype(F32)
    for i in range(2):
        for h in range(2):
            ga_ref[i, :, 128 * h : 128 * h + 128] = total[32 * i + 16 * h : 32 * i + 16 * h + 16]
            k = 2 * i + h
            gb_ref[i, 8 * h : 8 * h + 8, :] = total[64:72, 32 * k : 32 * k + 32]


def shards(activations, out_grads, tile_domain, adapter_a, adapter_b):
    shape = jax.ShapeDtypeStruct
    ids = tile_domain[:, 0]
    og = out_grads.T
    pair = [(f, f ^ 1) for f in range(2 * DEPTH)]
    columns = [[2 * z + c for z in range(DEPTH)] for c in range(2)]
    along_z = lambda x: lax.all_to_all(x, "fsdp", 0, 0, tiled=True, axis_index_groups=columns)

    packed = call(pack_kernel, shape((OWNERS, ROWS, 128), BF16), [VMEM, VMEM], adapter_a, adapter_b)
    weights = lax.all_to_all(packed, "dp", 0, 0, tiled=True)
    part = shape((DEPTH, 32, 128), F32)
    keep, send = call(partial_kernel, (part, part), [SMEM, VMEM, VMEM, VMEM], ids, weights, activations, og)
    chip = keep + lax.ppermute(send, "fsdp", pair)
    full = call(round_kernel, shape((DEPTH, 32, 128), BF16), [VMEM], along_z(chip))
    own = along_z(full)
    other = lax.ppermute(own, "fsdp", pair)
    grads = call(
        grad_kernel,
        shape((OWNERS, ROWS, 128), BF16),
        [SMEM, VMEM, VMEM, VMEM, VMEM],
        ids,
        activations,
        og,
        own,
        other,
        scratch=[
            pltpu.VMEM((OWNERS, ROWS, 128), F32),
            pltpu.VMEM((2 * DEPTH, 16, 256), F32),
            pltpu.VMEM((2 * DEPTH, 16, 128), F32),
        ],
    )
    summed = lax.all_to_all(grads, "dp", 0, 0, tiled=True)
    return call(final_kernel, (shape((2, RANK, 256), F32), shape((2, RANK, 32), F32)), [VMEM], summed)


def solution(mesh):
    placed = (
        P("dp", "fsdp"),
        P("dp", "fsdp"),
        P("dp", None),
        P("dp", None, "fsdp"),
        P("dp", None, "fsdp"),
    )
    return jax.shard_map(
        shards,
        mesh=mesh,
        in_specs=placed,
        out_specs=(P("dp", None, "fsdp"), P("dp", None, "fsdp")),
        check_vma=False,
    )
```

time: 406 us -> 127 us (0.31)
  the two profiles are of different devices: /device:TPU:16 before, /device:TPU:8 now
where the time goes in v1:
time: 127 us; the launch traced here: 126 us
  blocking collectives  110 us (87%)
  local copies, waits for them, and re-layouts  4.61 us (4%)
  Pallas kernels  4 us (3%)
  starting transfers between devices  3.84 us (3%)
  waiting for transfers between devices  2.81 us (2%)
    all_to_all x2, blocking collectives, shards(): lax.all_to_all(x, 'fsdp', 0, 0, tiled=True, axis_index_groups=columns)  56.7 us
    all_to_all x1, blocking collectives, shards(): weights = lax.all_to_all(packed, 'dp', 0, 0, tiled=True)  29.5 us
    all_to_all x1, blocking collectives, shards(): summed = lax.all_to_all(grads, 'dp', 0, 0, tiled=True)  23.9 us
    unnamed x16, local copies, waits for them, and re-layouts  4.61 us
    pallas_call x5, Pallas kernels, call(): pl.pallas_call(kernel, out_shape=out, in_specs=specs, out_specs=jax.tree....  4 us
  transfers between devices with their start and end apart: 2, of which 2 were waited for; matrix products, arithmetic and copies ran while one was open for 0% of the time, Pallas kernels for 0%

profile of v1, /device:TPU:8, one launch (start us, length us, event | category | flops | bytes accessed | tf_op | source)
XLA Modules:
  0.0 126.1 jit_solution(4692537355314939460)
XLA Ops:
  0.6 0.0 copy-start.4
  0.6 0.7 copy-done.4
  1.3 0.0 copy-start.5
  1.4 0.7 copy-done.5
  2.0 0.1 shard_map.68
  2.2 29.5 %all_to_all.20.w_ref = bf16[32,72,128]{2,1,0:T(8,128)(2,1)S(1)} all-to-all(bf16[32,72,128]{2,1,0:T(8,128)(2,1)S(1)} %shard_map.68), channel_id=1, replica_groups=mesh['dp'=32,'fsdp'=32] {'dp'}, dimensions={0} | all-to-all | bytes 1179648 | tf_op jit(solution)/shard_map/all_to_all | solution.py:141
  31.7 0.0 copy-start
  31.7 1.6 %copy-done = bf16[4096,256]{1,0:T(8,128)(2,1)S(1)} copy-done((bf16[4096,256]{1,0:T(8,128)(2,1)S(1)}, bf16[4096,256]{1,0:T(8,128)(2,1)}, u32[]{:S(2)}) %copy-start) | copy-done | bytes 2097176
  33.3 0.0 copy-start.2
  33.3 0.9 copy-done.2
  34.2 0.0 copy-start.6
  34.3 0.7 copy-done.6
  34.9 0.0 copy-start.1
  34.9 0.0 copy-start.3
  34.9 0.0 copy-start.7
  34.9 1.5 %shard_map.69 = (f32[16,32,128]{2,1,0:T(8,128)S(1)}, f32[16,32,128]{2,1,0:T(8,128)S(1)}) custom-call(s32[32]{0:T(128)S(1)} %bitcast.4, bf16[32,72,128]{2,1,0:T(8,128)(2,1)S(1)} %all_to_all.20.w_ref, bf16[4096,256]{1,0:T(8,128)(2,1)S(1)} %copy-done, bf16[32,4096]{1,0:T(8,128)(2,1)S(1)} %bitcast.2), custom_call_target="tpu_custom_call" | custom-call | tf_op jit(solution)/shard_map/pallas_call | solution.py:24
  36.4 1.9 %collective-permute-start = (f32[16,32,128]{2,1,0:T(8,128)S(1)}, f32[16,32,128]{2,1,0:T(8,128)S(1)}, u32[]{:S(2)}, u32[]{:S(2)}) collective-permute-start(f32[16,32,128]{2,1,0:T(8,128)S(1)} %get-tuple-element.5), channel_id=1, source_target_pairs={{0,1},{1,0},{2,3},{3,2},{4,5},{5,4},{6,7},{7,6},{8,9},{9,8},{10,11... | collective-permute-start | bytes 786440 | tf_op jit(solution)/shard_map/ppermute | solution.py:144
  38.4 1.5 %collective-permute-done = f32[16,32,128]{2,1,0:T(8,128)S(1)} collective-permute-done((f32[16,32,128]{2,1,0:T(8,128)S(1)}, f32[16,32,128]{2,1,0:T(8,128)S(1)}, u32[]{:S(2)}, u32[]{:S(2)}) %collective-permute-start) | collective-permute-done | bytes 262176 | tf_op jit(solution)/shard_map/ppermute | solution.py:144
  39.9 36.1 %all_to_all.21.in_ref = f32[16,32,128]{2,1,0:T(8,128)S(1)} all-to-all(f32[16,32,128]{2,1,0:T(8,128)S(1)} %add.3), channel_id=1, replica_groups={{0,2,4,6,8,10,12,14,16,18,20,22,24,26,28,30},{1,3,5,7,9,11,13,15,17,19,..., dimensions={0} | all-to-all | bytes 524288 | tf_op jit(solution)/shard_map/all_to_all | solution.py:138
  76.1 20.5 %all_to_all.22.own_ref = bf16[16,32,128]{2,1,0:T(8,128)(2,1)S(1)} all-to-all(bf16[16,32,128]{2,1,0:T(8,128)(2,1)S(1)} %shard_map.70), channel_id=1, replica_groups={{0,2,4,6,8,10,12,14,16,18,20,22,24,26,28,30},{1,3,5,7,9,11,13,15,17,19,..., dimensions={0} | all-to-all | bytes 262144 | tf_op jit(solution)/shard_map/all_to_all | solution.py:138
  96.6 1.9 %collective-permute-start.1 = (bf16[16,32,128]{2,1,0:T(8,128)(2,1)S(1)}, bf16[16,32,128]{2,1,0:T(8,128)(2,1)S(1)}, u32[]{:S(2)}, u32[]{:S(2)}) collective-permute-start(bf16[16,32,128]{2,1,0:T(8,128)(2,1)S(1)} %all_to_all.22.own_ref), channel_id=1, source_target_pairs={{0,1},{1,0},{2,3},{3,2},{4,5},{5,4},{6,7},{7,6},{8,9},{9,8},{10,11... | collective-permute-start | bytes 393224 | tf_op jit(solution)/shard_map/ppermute | solution.py:147
  98.5 1.3 %collective-permute-done.1.other_ref = bf16[16,32,128]{2,1,0:T(8,128)(2,1)S(1)} collective-permute-done((bf16[16,32,128]{2,1,0:T(8,128)(2,1)S(1)}, bf16[16,32,128]{2,1,0:T(8,128)(2,1)S(1)}, u32[]{:S(2)}, u32[]{:S(2)}) %collective-permute-start.1) | collective-permute-done | bytes 131104 | tf_op jit(solution)/shard_map/ppermute | solution.py:147
  99.8 0.0 copy-done.1
  99.8 0.0 copy-done.3
  99.8 0.0 copy-done.7
  99.8 1.6 %shard_map.71 = bf16[32,72,128]{2,1,0:T(8,128)(2,1)S(1)} custom-call(s32[32]{0:T(128)S(1)} %bitcast.5, bf16[4096,256]{1,0:T(8,128)(2,1)S(1)} %copy-done.1, bf16[32,4096]{1,0:T(8,128)(2,1)S(1)} %bitcast.3, bf16[16,32,128]{2,1,0:T(8,128)(2,1)S(1)} %all_to_all.22.own_ref, bf16[16,32,128]{2,1,0:T(8,128)(2,1)S(1)} %collective-permute-done.1.other_ref), custom_call_target="tpu_custom_call" | custom-call | tf_op jit(solution)/shard_map/pallas_call | solution.py:24
  101.5 23.9 %all_to_all.23.in_ref = bf16[32,72,128]{2,1,0:T(8,128)(2,1)S(1)} all-to-all(bf16[32,72,128]{2,1,0:T(8,128)(2,1)S(1)} %shard_map.71), channel_id=1, replica_groups=mesh['dp'=32,'fsdp'=32] {'dp'}, dimensions={0} | all-to-all | bytes 1179648 | tf_op jit(solution)/shard_map/all_to_all | solution.py:163
  125.4 0.7 shard_map.72
  (2 shorter events, 0.1 us)
Async XLA Ops:
  0.6 0.7 copy-start.4
  1.3 0.7 copy-start.5
  31.7 1.6 %copy-start = (bf16[4096,256]{1,0:T(8,128)(2,1)S(1)}, bf16[4096,256]{1,0:T(8,128)(2,1)}, u32[]{:S(2)}) copy-start(bf16[4096,256]{1,0:T(8,128)(2,1)} %act_ref.3) | copy-start | bytes 6291460
  33.3 0.9 copy-start.2
  34.2 0.7 copy-start.6
  34.9 64.9 %copy-start.1 = (bf16[4096,256]{1,0:T(8,128)(2,1)S(1)}, bf16[4096,256]{1,0:T(8,128)(2,1)}, u32[]{:S(2)}) copy-start(bf16[4096,256]{1,0:T(8,128)(2,1)} %act_ref.3) | copy-start | bytes 6291460
  34.9 64.9 %copy-start.3 = (bf16[4096,32]{0,1:T(8,128)(2,1)S(1)}, bf16[4096,32]{0,1:T(8,128)(2,1)}, u32[]{:S(2)}) copy-start(bf16[4096,32]{0,1:T(8,128)(2,1)} %param.6) | copy-start | bytes 786436
  34.9 64.9 %copy-start.7 = (s32[32,1]{0,1:T(1,128)S(1)}, s32[32,1]{0,1:T(1,128)}, u32[]{:S(2)}) copy-start(s32[32,1]{0,1:T(1,128)} %param.7) | copy-start | bytes 388
  36.4 3.4 %collective-permute-start = (f32[16,32,128]{2,1,0:T(8,128)S(1)}, f32[16,32,128]{2,1,0:T(8,128)S(1)}, u32[]{:S(2)}, u32[]{:S(2)}) collective-permute-start(f32[16,32,128]{2,1,0:T(8,128)S(1)} %get-tuple-element.5), channel_id=1, source_target_pairs={{0,1},{1,0},{2,3},{3,2},{4,5},{5,4},{6,7},{7,6},{8,9},{9,8},{10,11... | collective-permute-start | bytes 786440 | tf_op jit(solution)/shard_map/ppermute | solution.py:144
  96.6 3.2 %collective-permute-start.1 = (bf16[16,32,128]{2,1,0:T(8,128)(2,1)S(1)}, bf16[16,32,128]{2,1,0:T(8,128)(2,1)S(1)}, u32[]{:S(2)}, u32[]{:S(2)}) collective-permute-start(bf16[16,32,128]{2,1,0:T(8,128)(2,1)S(1)} %all_to_all.22.own_ref), channel_id=1, source_target_pairs={{0,1},{1,0},{2,3},{3,2},{4,5},{5,4},{6,7},{7,6},{8,9},{9,8},{10,11... | collective-permute-start | bytes 393224 | tf_op jit(solution)/shard_map/ppermute | solution.py:147

commit v2 on v1

v2 whole, which is shorter than its diff:
```python
import jax
import jax.numpy as jnp
from jax import lax
from jax.experimental import pallas as pl
from jax.experimental.pallas import tpu as pltpu
from jax.sharding import PartitionSpec as P

F32 = jnp.float32
BF16 = jnp.bfloat16
F16 = jnp.float16
TILE = 128
RANK = 16
OWNERS = 32
NEAR = 8
FAR = 4
TILES = NEAR * FAR
ROWS = 72
SENT = FAR * 32 + 8
TOP = 16384.0

NT = (((1,), (1,)), ((), ()))
NN = (((1,), (0,)), ((), ()))
VMEM = pl.BlockSpec(memory_space=pltpu.VMEM)
SMEM = pl.BlockSpec(memory_space=pltpu.SMEM)
MIB = 1024 * 1024
AHEAD = pl.CostEstimate(flops=10_000_000_000, bytes_accessed=20_000_000, transcendentals=0)


def call(kernel, out, specs, *operands, scratch=(), cost=None):
    return pl.pallas_call(
        kernel,
        out_shape=out,
        in_specs=specs,
        out_specs=jax.tree.map(lambda _: VMEM, out),
        scratch_shapes=scratch,
        cost_estimate=cost,
        compiler_params=pltpu.CompilerParams(vmem_limit_bytes=32 * MIB),
    )(*operands)


def lane_block():
    return lax.broadcasted_iota(jnp.int32, (8, 128), 1) // 32


def pack_kernel(a_ref, b_ref, out_ref):
    pieces = []
    for i in range(2):
        pieces += [a_ref[i, :, 0:128], a_ref[i, :, 128:256]]
    rows = lax.broadcasted_iota(jnp.int32, (32, 128), 0)
    lanes = lax.broadcasted_iota(jnp.int32, (32, 128), 1)
    small = jnp.zeros((8, 128), F32)
    for i in range(2):
        for h in range(2):
            place = jnp.where(lanes == rows + 32 * (2 * i + h), 1.0, 0.0).astype(BF16)
            spread = lax.dot_general(b_ref[i], place, NN, preferred_element_type=F32)
            small = small + spread[8 * h : 8 * h + 8]
    big = jnp.concatenate(pieces, axis=0)
    small = small.astype(BF16)
    for o in range(OWNERS):
        out_ref[o, 0:64] = big
        out_ref[o, 64:72] = small


def tile_og(og_ref, tile):
    og = og_ref[:, tile * TILE : tile * TILE + TILE]
    return jnp.concatenate([og, og, og, og], axis=0)


def tile_act(act_ref, tile):
    return act_ref[tile * TILE : tile * TILE + TILE, :]


def scale_of(down_top, up_top):
    down = jnp.broadcast_to(jnp.max(down_top, axis=(0, 1), keepdims=True), (8, 128))
    up = jnp.broadcast_to(jnp.max(up_top, axis=(0, 1), keepdims=True), (8, 128))
    both = jnp.where(lax.broadcasted_iota(jnp.int32, (8, 128), 0) == 0, down, up)
    root = jnp.sqrt(jnp.sqrt(both))
    return jnp.maximum(root, 2.0**-13).astype(BF16).astype(F32)


def fourth(root):
    square = root * root
    return square * square


def widen(row):
    return jnp.broadcast_to(row, (16, 128))


def partial_kernel(ids_ref, w_ref, act_ref, og_ref, out_ref, part_ref):
    block = lane_block()
    down_top = jnp.zeros((RANK, TILE), F32)
    up_top = jnp.zeros((RANK, TILE), F32)
    for tile in range(TILES):
        e = ids_ref[tile]
        o = e // 2
        i = e % 2
        a = w_ref[o, pl.ds(pl.multiple_of(i * 32, 32), 32), :]
        b = w_ref[o, 64:72, :].astype(F32)
        left = jnp.concatenate([a[0:16], a[16:32]], axis=1)
        down = lax.dot_general(left, tile_act(act_ref, tile), NT, preferred_element_type=F32)
        spread = jnp.concatenate(
            [jnp.where(block == 2 * i, b, 0.0), jnp.where(block == 2 * i + 1, b, 0.0)], axis=0
        ).astype(BF16)
        up = lax.dot_general(spread, tile_og(og_ref, tile), NN, preferred_element_type=F32)
        part_ref[tile, 0:16] = down
        part_ref[tile, 16:32] = up
        down_top = jnp.maximum(down_top, jnp.abs(down))
        up_top = jnp.maximum(up_top, jnp.abs(up))
    root = scale_of(down_top, up_top)
    factor = TOP / fourth(root)
    down_factor, up_factor = widen(factor[0:1]), widen(factor[1:2])
    for q in range(NEAR):
        for a in range(FAR):
            tile = NEAR * a + q
            out_ref[q, 32 * a : 32 * a + 16] = part_ref[tile, 0:16] * down_factor
            out_ref[q, 32 * a + 16 : 32 * a + 32] = part_ref[tile, 16:32] * up_factor
        out_ref[q, FAR * 32 : SENT] = root


def summed_parts(in_ref, count):
    downs = [jnp.zeros((RANK, TILE), F32)] * FAR
    ups = [jnp.zeros((RANK, TILE), F32)] * FAR
    for q in range(count):
        factor = fourth(in_ref[q, FAR * 32 : SENT]) * (1.0 / TOP)
        down_factor, up_factor = widen(factor[0:1]), widen(factor[1:2])
        for a in range(FAR):
            downs[a] = downs[a] + in_ref[q, 32 * a : 32 * a + 16] * down_factor
            ups[a] = ups[a] + in_ref[q, 32 * a + 16 : 32 * a + 32] * up_factor
    return downs, ups


def near_kernel(in_ref, out_ref):
    downs, ups = summed_parts(in_ref, NEAR)
    down_top, up_top = jnp.abs(downs[0]), jnp.abs(ups[0])
    for a in range(1, FAR):
        down_top = jnp.maximum(down_top, jnp.abs(downs[a]))
        up_top = jnp.maximum(up_top, jnp.abs(ups[a]))
    root = scale_of(down_top, up_top)
    factor = TOP / fourth(root)
    down_factor, up_factor = widen(factor[0:1]), widen(factor[1:2])
    for a in range(FAR):
        down = downs[a] * down_factor
        up = ups[a] * up_factor
        for f in range(FAR):
            out_ref[f, 32 * a : 32 * a + 16] = down
            out_ref[f, 32 * a + 16 : 32 * a + 32] = up
    for f in range(FAR):
        out_ref[f, FAR * 32 : SENT] = root


def round_kernel(in_ref, out_ref):
    downs, ups = summed_parts(in_ref, FAR)
    for a in range(FAR):
        down = downs[a].astype(BF16)
        up = ups[a].astype(BF16)
        for q in range(NEAR):
            out_ref[q, 32 * a : 32 * a + 16] = down
            out_ref[q, 32 * a + 16 : 32 * a + 32] = up


def grad_kernel(ids_ref, act_ref, og_ref, in_ref, out_ref, acc_ref, ga_ref, gb_ref):
    acc_ref[...] = jnp.zeros_like(acc_ref)
    block = lane_block()
    for tile in range(TILES):
        q, a = tile % NEAR, tile // NEAR
        down = in_ref[q, 32 * a : 32 * a + 16]
        up = in_ref[q, 32 * a + 16 : 32 * a + 32]
        ga_ref[tile] = lax.dot_general(up, tile_act(act_ref, tile), NN, preferred_element_type=F32)
        gb_ref[tile] = lax.dot_general(down, tile_og(og_ref, tile), NT, preferred_element_type=F32)
    for tile in range(TILES):
        e = ids_ref[tile]
        o = e // 2
        i = e % 2
        ga = ga_ref[tile]
        gb = gb_ref[tile]
        at = pl.ds(pl.multiple_of(i * 32, 32), 32)
        acc_ref[o, at, :] += jnp.concatenate([ga[:, 0:128], ga[:, 128:256]], axis=0)
        acc_ref[o, 64:72, :] += jnp.where(block == 2 * i, gb[0:8], 0.0) + jnp.where(block == 2 * i + 1, gb[8:16], 0.0)
    for o in range(OWNERS):
        out_ref[o] = (2.0 * acc_ref[o]).astype(BF16)


def final_kernel(in_ref, ga_ref, gb_ref):
    total = in_ref[0].astype(F32)
    for o in range(1, OWNERS):
        total = total + in_ref[o].astype(F32)
    for i in range(2):
        for h in range(2):
            ga_ref[i, :, 128 * h : 128 * h + 128] = total[32 * i + 16 * h : 32 * i + 16 * h + 16]
            k = 2 * i + h
            gb_ref[i, 8 * h : 8 * h + 8, :] = total[64:72, 32 * k : 32 * k + 32]


def shards(activations, out_grads, tile_domain, adapter_a, adapter_b):
    shape = jax.ShapeDtypeStruct
    ids = tile_domain[:, 0]
    og = out_grads.T
    near_groups = [[NEAR * f + q for q in range(NEAR)] for f in range(FAR)]
    far_groups = [[NEAR * f + q for f in range(FAR)] for q in range(NEAR)]
    near = lambda x: lax.all_to_all(x, "fsdp", 0, 0, tiled=True, axis_index_groups=near_groups)
    far = lambda x: lax.all_to_all(x, "fsdp", 0, 0, tiled=True, axis_index_groups=far_groups)

    packed = call(
        pack_kernel,
        shape((OWNERS, ROWS, 128), BF16),
        [VMEM, VMEM],
        adapter_a,
        adapter_b,
        cost=AHEAD,
    )
    weights = lax.all_to_all(packed, "dp", 0, 0, tiled=True)
    part = call(
        partial_kernel,
        shape((NEAR, SENT, 128), F32),
        [SMEM, VMEM, VMEM, VMEM],
        ids,
        weights,
        activations,
        og,
        scratch=[pltpu.VMEM((TILES, 32, 128), F32)],
    )
    part = near(part.astype(F16)).astype(F32)
    part = call(near_kernel, shape((FAR, SENT, 128), F32), [VMEM], part)
    part = far(part.astype(F16)).astype(F32)
    full = near(call(round_kernel, shape((NEAR, FAR * 32, 128), BF16), [VMEM], part))
    grads = call(
        grad_kernel,
        shape((OWNERS, ROWS, 128), BF16),
        [SMEM, VMEM, VMEM, VMEM],
        ids,
        activations,
        og,
        full,
        scratch=[
            pltpu.VMEM((OWNERS, ROWS, 128), F32),
            pltpu.VMEM((TILES, 16, 256), F32),
            pltpu.VMEM((TILES, 16, 128), F32),
        ],
    )
    summed = lax.all_to_all(grads, "dp", 0, 0, tiled=True)
    return call(final_kernel, (shape((2, RANK, 256), F32), shape((2, RANK, 32), F32)), [VMEM], summed)


def solution(mesh):
    placed = (
        P("dp", "fsdp"),
        P("dp", "fsdp"),
        P("dp", None),
        P("dp", None, "fsdp"),
        P("dp", None, "fsdp"),
    )
    return jax.shard_map(
        shards,
        mesh=mesh,
        in_specs=placed,
        out_specs=(P("dp", None, "fsdp"), P("dp", None, "fsdp")),
        check_vma=False,
    )
```

time: 127 us -> 120 us (0.945)
  starting transfers between devices: 3.84 us -> 0 us
  local copies, waits for them, and re-layouts: 4.61 us -> 1.42 us
  blocking collectives: 110 us -> 113 us
  waiting for transfers between devices: 2.81 us -> 0 us
    ppermute x2 -> x0, starting transfers between devices: 3.84 us -> none  [the longest x1 1.93 us: shards(): chip = keep + lax.ppermute(send, 'fsdp', pair)]
    all_to_all x2 -> x3, blocking collectives: 56.7 us -> 60.3 us  [the longest x1 31.2 us: shards(): lax.all_to_all(x, 'fsdp', 0, 0, tiled=True, axis_index_groups=far_groups)]
    unnamed x16 -> x10, local copies, waits for them, and re-layouts: 4.61 us -> 1.42 us
    ppermute x2 -> x0, waiting for transfers between devices: 2.81 us -> none  [the longest x1 1.5 us: shards(): chip = keep + lax.ppermute(send, 'fsdp', pair)]
    pallas_call x5 -> x6, Pallas kernels: 4 us -> 4.39 us  [call(): pl.pallas_call(kernel, out_shape=out, in_specs=specs, out_specs=jax.tree....]
  transfers between devices with their start and end apart: 2 -> 0, of which waited for: 2 -> 0; matrix products, arithmetic and copies ran while one was open for 0% -> 0% of each run, Pallas kernels for 0% -> 0%
where the time goes in v2:
time: 120 us
  blocking collectives  113 us (94%)
  Pallas kernels  4.39 us (4%)
  local copies, waits for them, and re-layouts  1.42 us (1%)
    all_to_all x1, blocking collectives, shards(): lax.all_to_all(x, 'fsdp', 0, 0, tiled=True, axis_index_groups=far_groups)  31.2 us
    all_to_all x1, blocking collectives, shards(): weights = lax.all_to_all(packed, 'dp', 0, 0, tiled=True)  29.7 us
    all_to_all x2, blocking collectives, shards(): lax.all_to_all(x, 'fsdp', 0, 0, tiled=True, axis_index_groups=near_groups)  29.2 us
    all_to_all x1, blocking collectives, shards(): summed = lax.all_to_all(grads, 'dp', 0, 0, tiled=True)  23.2 us
    pallas_call x6, Pallas kernels, call(): pl.pallas_call(kernel, out_shape=out, in_specs=specs, out_specs=jax.tree....  4.39 us

profile of v2, /device:TPU:8, one launch (start us, length us, event | category | flops | bytes accessed | tf_op | source)
XLA Modules:
  0.0 119.9 jit_solution(13220017998782504034)
XLA Ops:
  0.6 0.0 copy-start.2
  0.6 0.0 copy-start.3
  0.7 0.7 copy-done.3
  1.4 0.0 copy-start.4
  1.4 0.7 copy-done.4
  2.1 0.0 copy-start
  2.1 0.0 copy-start.1
  2.1 0.1 shard_map.68
  2.2 29.7 %all_to_all.25.w_ref = bf16[32,72,128]{2,1,0:T(8,128)(2,1)S(1)} all-to-all(bf16[32,72,128]{2,1,0:T(8,128)(2,1)S(1)} %shard_map.68), channel_id=1, replica_groups=mesh['dp'=32,'fsdp'=32] {'dp'}, dimensions={0} | all-to-all | bytes 1179648 | tf_op jit(solution)/shard_map/all_to_all | solution.py:212
  31.9 0.0 copy-done.2
  31.9 0.0 copy-done
  31.9 0.0 copy-done.1
  31.9 1.7 %shard_map.69 = f32[8,136,128]{2,1,0:T(8,128)S(1)} custom-call(s32[32]{0:T(128)S(1)} %bitcast.4, bf16[32,72,128]{2,1,0:T(8,128)(2,1)S(1)} %all_to_all.25.w_ref, bf16[4096,256]{1,0:T(8,128)(2,1)S(1)} %copy-done, bf16[32,4096]{1,0:T(8,128)(2,1)S(1)} %bitcast.2), custom_call_target="tpu_custom_call" | custom-call | tf_op jit(solution)/shard_map/pallas_call | solution.py:30
  33.6 16.1 %all_to_all.26 = f16[8,136,128]{2,1,0:T(8,128)(2,1)S(1)} all-to-all(f16[8,136,128]{2,1,0:T(8,128)(2,1)S(1)} %convert_element_type.12), channel_id=1, replica_groups={{0,1,2,3,4,5,6,7},{8,9,10,11,12,13,14,15},{16,17,18,19,20,21,22,23},{24..., dimensions={0} | all-to-all | bytes 557056 | tf_op jit(solution)/shard_map/all_to_all | solution.py:201
  49.8 0.2 shard_map.70
  50.0 31.2 %all_to_all.27 = f16[4,136,128]{2,1,0:T(8,128)(2,1)S(1)} all-to-all(f16[4,136,128]{2,1,0:T(8,128)(2,1)S(1)} %convert_element_type.14), channel_id=1, replica_groups={{0,8,16,24},{1,9,17,25},{2,10,18,26},{3,11,19,27},{4,12,20,28},{5,13,21..., dimensions={0} | all-to-all | bytes 278528 | tf_op jit(solution)/shard_map/all_to_all | solution.py:202
  81.2 13.1 %all_to_all.28.in_ref = bf16[8,128,128]{2,1,0:T(8,128)(2,1)S(1)} all-to-all(bf16[8,128,128]{2,1,0:T(8,128)(2,1)S(1)} %shard_map.71), channel_id=1, replica_groups={{0,1,2,3,4,5,6,7},{8,9,10,11,12,13,14,15},{16,17,18,19,20,21,22,23},{24..., dimensions={0} | all-to-all | bytes 524288 | tf_op jit(solution)/shard_map/all_to_all | solution.py:201
  94.3 1.6 %shard_map.72 = bf16[32,72,128]{2,1,0:T(8,128)(2,1)S(1)} custom-call(s32[32]{0:T(128)S(1)} %bitcast.5, bf16[4096,256]{1,0:T(8,128)(2,1)S(1)} %copy-done, bf16[32,4096]{1,0:T(8,128)(2,1)S(1)} %bitcast.3, bf16[8,128,128]{2,1,0:T(8,128)(2,1)S(1)} %all_to_all.28.in_ref), custom_call_target="tpu_custom_call" | custom-call | tf_op jit(solution)/shard_map/pallas_call | solution.py:30
  95.9 23.2 %all_to_all.29.in_ref = bf16[32,72,128]{2,1,0:T(8,128)(2,1)S(1)} all-to-all(bf16[32,72,128]{2,1,0:T(8,128)(2,1)S(1)} %shard_map.72), channel_id=1, replica_groups=mesh['dp'=32,'fsdp'=32] {'dp'}, dimensions={0} | all-to-all | bytes 1179648 | tf_op jit(solution)/shard_map/all_to_all | solution.py:241
  119.2 0.7 shard_map.73
  (5 shorter events, 0.1 us)
Async XLA Ops:
  0.6 31.2 %copy-start.2 = (s32[32,1]{0,1:T(1,128)S(1)}, s32[32,1]{0,1:T(1,128)}, u32[]{:S(2)}) copy-start(s32[32,1]{0,1:T(1,128)} %param.7) | copy-start | bytes 388
  0.6 0.7 copy-start.3
  1.4 0.7 copy-start.4
  2.1 29.8 %copy-start = (bf16[4096,256]{1,0:T(8,128)(2,1)S(1)}, bf16[4096,256]{1,0:T(8,128)(2,1)}, u32[]{:S(2)}) copy-start(bf16[4096,256]{1,0:T(8,128)(2,1)} %act_ref.3) | copy-start | bytes 6291460
  2.1 29.8 %copy-start.1 = (bf16[4096,32]{0,1:T(8,128)(2,1)S(1)}, bf16[4096,32]{0,1:T(8,128)(2,1)}, u32[]{:S(2)}) copy-start(bf16[4096,32]{0,1:T(8,128)(2,1)} %param.6) | copy-start | bytes 786436

commit v3 on v2

--- a/solution.py
+++ b/solution.py
@@ -1,3 +1,5 @@
+import functools
+
 import jax
 import jax.numpy as jnp
 from jax import lax
@@ -11,9 +13,9 @@
 TILE = 128
 RANK = 16
 OWNERS = 32
-NEAR = 8
+NEAR = 4
 FAR = 4
-TILES = NEAR * FAR
+SHARE = NEAR * FAR
 ROWS = 72
 SENT = FAR * 32 + 8
 TOP = 16384.0
@@ -24,6 +26,7 @@
 SMEM = pl.BlockSpec(memory_space=pltpu.SMEM)
 MIB = 1024 * 1024
 AHEAD = pl.CostEstimate(flops=10_000_000_000, bytes_accessed=20_000_000, transcendentals=0)
+HALF = pl.CostEstimate(flops=2_000_000_000, bytes_accessed=4_000_000, transcendentals=0)
 
 
 def call(kernel, out, specs, *operands, scratch=(), cost=None):
@@ -61,13 +64,17 @@
         out_ref[o, 64:72] = small
 
 
+def tile_at(b, a, parity):
+    return 2 * NEAR * a + 2 * b + parity
+
+
 def tile_og(og_ref, tile):
-    og = og_ref[:, tile * TILE : tile * TILE + TILE]
+    og = og_ref[:, pl.ds(pl.multiple_of(tile * TILE, TILE), TILE)]
     return jnp.concatenate([og, og, og, og], axis=0)
 
 
 def tile_act(act_ref, tile):
-    return act_ref[tile * TILE : tile * TILE + TILE, :]
+    return act_ref[pl.ds(pl.multiple_of(tile * TILE, TILE), TILE), :]
 
 
 def scale_of(down_top, up_top):
@@ -87,35 +94,47 @@
     return jnp.broadcast_to(row, (16, 128))
 
 
-def partial_kernel(ids_ref, w_ref, act_ref, og_ref, out_ref, part_ref):
+def parity_of(own):
+    core = lax.axis_index("fsdp") % 2
+    return core if own else 1 - core
+
+
+def partial_kernel(own, ids_ref, w_ref, act_ref, og_ref, out_ref):
+    parity = parity_of(own)
     block = lane_block()
+    for b in range(NEAR):
+        for a in range(FAR):
+            tile = tile_at(b, a, parity)
+            e = ids_ref[tile]
+            o = e // 2
+            i = e % 2
+            w = w_ref[o, pl.ds(pl.multiple_of(i * 32, 32), 32), :]
+            small = w_ref[o, 64:72, :].astype(F32)
+            left = jnp.concatenate([w[0:16], w[16:32]], axis=1)
+            down = lax.dot_general(left, tile_act(act_ref, tile), NT, preferred_element_type=F32)
+            spread = jnp.concatenate(
+                [jnp.where(block == 2 * i, small, 0.0), jnp.where(block == 2 * i + 1, small, 0.0)], axis=0
+            ).astype(BF16)
+            up = lax.dot_general(spread, tile_og(og_ref, tile), NN, preferred_element_type=F32)
+            out_ref[b, 32 * a : 32 * a + 16] = down
+            out_ref[b, 32 * a + 16 : 32 * a + 32] = up
+
+
+def chip_kernel(keep_ref, other_ref, out_ref, part_ref):
     down_top = jnp.zeros((RANK, TILE), F32)
     up_top = jnp.zeros((RANK, TILE), F32)
-    for tile in range(TILES):
-        e = ids_ref[tile]
-        o = e // 2
-        i = e % 2
-        a = w_ref[o, pl.ds(pl.multiple_of(i * 32, 32), 32), :]
-        b = w_ref[o, 64:72, :].astype(F32)
-        left = jnp.concatenate([a[0:16], a[16:32]], axis=1)
-        down = lax.dot_general(left, tile_act(act_ref, tile), NT, preferred_element_type=F32)
-        spread = jnp.concatenate(
-            [jnp.where(block == 2 * i, b, 0.0), jnp.where(block == 2 * i + 1, b, 0.0)], axis=0
-        ).astype(BF16)
-        up = lax.dot_general(spread, tile_og(og_ref, tile), NN, preferred_element_type=F32)
-        part_ref[tile, 0:16] = down
-        part_ref[tile, 16:32] = up
-        down_top = jnp.maximum(down_top, jnp.abs(down))
-        up_top = jnp.maximum(up_top, jnp.abs(up))
+    for b in range(NEAR):
+        part = keep_ref[b] + other_ref[b]
+        part_ref[b] = part
+        for a in range(FAR):
+            down_top = jnp.maximum(down_top, jnp.abs(part[32 * a : 32 * a + 16]))
+            up_top = jnp.maximum(up_top, jnp.abs(part[32 * a + 16 : 32 * a + 32]))
     root = scale_of(down_top, up_top)
     factor = TOP / fourth(root)
-    down_factor, up_factor = widen(factor[0:1]), widen(factor[1:2])
-    for q in range(NEAR):
-        for a in range(FAR):
-            tile = NEAR * a + q
-            out_ref[q, 32 * a : 32 * a + 16] = part_ref[tile, 0:16] * down_factor
-            out_ref[q, 32 * a + 16 : 32 * a + 32] = part_ref[tile, 16:32] * up_factor
-        out_ref[q, FAR * 32 : SENT] = root
+    both = jnp.concatenate([widen(factor[0:1]), widen(factor[1:2])] * FAR, axis=0)
+    for b in range(NEAR):
+        out_ref[b, 0 : FAR * 32] = part_ref[b] * both
+        out_ref[b, FAR * 32 : SENT] = root
 
 
 def summed_parts(in_ref, count):
@@ -159,24 +178,35 @@
             out_ref[q, 32 * a + 16 : 32 * a + 32] = up
 
 
-def grad_kernel(ids_ref, act_ref, og_ref, in_ref, out_ref, acc_ref, ga_ref, gb_ref):
-    acc_ref[...] = jnp.zeros_like(acc_ref)
+def add_grads(own, ids_ref, act_ref, og_ref, in_ref, acc_ref, ga_ref, gb_ref):
+    parity = parity_of(own)
     block = lane_block()
-    for tile in range(TILES):
-        q, a = tile % NEAR, tile // NEAR
-        down = in_ref[q, 32 * a : 32 * a + 16]
-        up = in_ref[q, 32 * a + 16 : 32 * a + 32]
-        ga_ref[tile] = lax.dot_general(up, tile_act(act_ref, tile), NN, preferred_element_type=F32)
-        gb_ref[tile] = lax.dot_general(down, tile_og(og_ref, tile), NT, preferred_element_type=F32)
-    for tile in range(TILES):
-        e = ids_ref[tile]
+    places = [(b, a) for b in range(NEAR) for a in range(FAR)]
+    for n, (b, a) in enumerate(places):
+        tile = tile_at(b, a, parity)
+        down = in_ref[b, 32 * a : 32 * a + 16]
+        up = in_ref[b, 32 * a + 16 : 32 * a + 32]
+        ga_ref[n] = lax.dot_general(up, tile_act(act_ref, tile), NN, preferred_element_type=F32)
+        gb_ref[n] = lax.dot_general(down, tile_og(og_ref, tile), NT, preferred_element_type=F32)
+    for n, (b, a) in enumerate(places):
+        e = ids_ref[tile_at(b, a, parity)]
         o = e // 2
         i = e % 2
-        ga = ga_ref[tile]
-        gb = gb_ref[tile]
+        ga = ga_ref[n]
+        gb = gb_ref[n]
         at = pl.ds(pl.multiple_of(i * 32, 32), 32)
         acc_ref[o, at, :] += jnp.concatenate([ga[:, 0:128], ga[:, 128:256]], axis=0)
         acc_ref[o, 64:72, :] += jnp.where(block == 2 * i, gb[0:8], 0.0) + jnp.where(block == 2 * i + 1, gb[8:16], 0.0)
+
+
+def first_kernel(ids_ref, act_ref, og_ref, in_ref, acc_ref, ga_ref, gb_ref):
+    acc_ref[...] = jnp.zeros_like(acc_ref)
+    add_grads(True, ids_ref, act_ref, og_ref, in_ref, acc_ref, ga_ref, gb_ref)
+
+
+def second_kernel(ids_ref, act_ref, og_ref, in_ref, sum_ref, out_ref, acc_ref, ga_ref, gb_ref):
+    acc_ref[...] = sum_ref[...]
+    add_grads(False, ids_ref, act_ref, og_ref, in_ref, acc_ref, ga_ref, gb_ref)
     for o in range(OWNERS):
         out_ref[o] = (2.0 * acc_ref[o]).astype(BF16)
 
@@ -196,10 +226,12 @@
     shape = jax.ShapeDtypeStruct
     ids = tile_domain[:, 0]
     og = out_grads.T
-    near_groups = [[NEAR * f + q for q in range(NEAR)] for f in range(FAR)]
-    far_groups = [[NEAR * f + q for f in range(FAR)] for q in range(NEAR)]
+    pair = [(f, f ^ 1) for f in range(2 * SHARE)]
+    near_groups = [[2 * (NEAR * a + b) + c for b in range(NEAR)] for a in range(FAR) for c in range(2)]
+    far_groups = [[2 * (NEAR * a + b) + c for a in range(FAR)] for b in range(NEAR) for c in range(2)]
     near = lambda x: lax.all_to_all(x, "fsdp", 0, 0, tiled=True, axis_index_groups=near_groups)
     far = lambda x: lax.all_to_all(x, "fsdp", 0, 0, tiled=True, axis_index_groups=far_groups)
+    swap = lambda x: lax.ppermute(x, "fsdp", pair)
 
     packed = call(
         pack_kernel,
@@ -210,33 +242,23 @@
         cost=AHEAD,
     )
     weights = lax.all_to_all(packed, "dp", 0, 0, tiled=True)
-    part = call(
-        partial_kernel,
-        shape((NEAR, SENT, 128), F32),
-        [SMEM, VMEM, VMEM, VMEM],
-        ids,
-        weights,
-        activations,
-        og,
-        scratch=[pltpu.VMEM((TILES, 32, 128), F32)],
-    )
-    part = near(part.astype(F16)).astype(F32)
-    part = call(near_kernel, shape((FAR, SENT, 128), F32), [VMEM], part)
+    inputs = (ids, weights, activations, og)
+    part = shape((NEAR, FAR * 32, 128), F32)
+    kinds = [SMEM, VMEM, VMEM, VMEM]
+    send = call(functools.partial(partial_kernel, False), part, kinds, *inputs, cost=HALF)
+    keep = call(functools.partial(partial_kernel, True), part, kinds, *inputs, cost=HALF)
+    scaled = shape((NEAR, SENT, 128), F32)
+    chip = call(chip_kernel, scaled, [VMEM, VMEM], keep, swap(send), scratch=[pltpu.VMEM(part.shape, F32)])
+    chip = near(chip.astype(F16)).astype(F32)
+    part = call(near_kernel, shape((FAR, SENT, 128), F32), [VMEM], chip)
     part = far(part.astype(F16)).astype(F32)
     full = near(call(round_kernel, shape((NEAR, FAR * 32, 128), BF16), [VMEM], part))
+    terms = [pltpu.VMEM((SHARE, 16, 256), F32), pltpu.VMEM((SHARE, 16, 128), F32)]
+    total = (OWNERS, ROWS, 128)
+    inputs = (ids, activations, og)
+    grads = call(first_kernel, shape(total, F32), kinds, *inputs, full, scratch=terms, cost=HALF)
     grads = call(
-        grad_kernel,
-        shape((OWNERS, ROWS, 128), BF16),
-        [SMEM, VMEM, VMEM, VMEM],
-        ids,
-        activations,
-        og,
-        full,
-        scratch=[
-            pltpu.VMEM((OWNERS, ROWS, 128), F32),
-            pltpu.VMEM((TILES, 16, 256), F32),
-            pltpu.VMEM((TILES, 16, 128), F32),
-        ],
+        second_kernel, shape(total, BF16), kinds + [VMEM], *inputs, swap(full), grads, scratch=[pltpu.VMEM(total, F32)] + terms
     )
     summed = lax.all_to_all(grads, "dp", 0, 0, tiled=True)
     return call(final_kernel, (shape((2, RANK, 256), F32), shape((2, RANK, 32), F32)), [VMEM], summed)

time: 120 us -> 119 us (level)
  the two profiles are of different devices: /device:TPU:8 before, /device:TPU:2 now
where the time goes in v3:
time: 119 us; the launch traced here: 118 us
  blocking collectives  106 us (89%)
  Pallas kernels  5.7 us (5%)
  starting transfers between devices  3.84 us (3%)
  local copies, waits for them, and re-layouts  1.57 us (1%)
    all_to_all x1, blocking collectives, shards(): lax.all_to_all(x, 'fsdp', 0, 0, tiled=True, axis_index_groups=far_groups)  30.7 us
    all_to_all x1, blocking collectives, shards(): weights = lax.all_to_all(packed, 'dp', 0, 0, tiled=True)  29.2 us
    all_to_all x1, blocking collectives, shards(): summed = lax.all_to_all(grads, 'dp', 0, 0, tiled=True)  24.1 us
    all_to_all x2, blocking collectives, shards(): lax.all_to_all(x, 'fsdp', 0, 0, tiled=True, axis_index_groups=near_groups)  21.6 us
    pallas_call x9, Pallas kernels, call(): pl.pallas_call(kernel, out_shape=out, in_specs=specs, out_specs=jax.tree....  5.7 us
    ppermute x2, starting transfers between devices, shards(): swap = lambda x: lax.ppermute(x, 'fsdp', pair)  3.84 us
  transfers between devices with their start and end apart: 2, of which 2 were waited for; matrix products, arithmetic and copies ran while one was open for 0% of the time, Pallas kernels for 2%

profile of v3, /device:TPU:2, one launch (start us, length us, event | category | flops | bytes accessed | tf_op | source)
XLA Modules:
  0.0 118.2 jit_solution(15370735295755108525)
XLA Ops:
  0.6 0.0 copy-start
  0.6 0.0 copy-start.2
  0.7 0.0 copy-start.3
  0.7 0.9 copy-done.3
  1.5 0.0 copy-start.4
  1.5 0.7 copy-done.4
  2.2 0.0 copy-start.1
  2.2 0.1 shard_map.68
  2.4 29.2 %all_to_all.25.w_ref = bf16[32,72,128]{2,1,0:T(8,128)(2,1)S(1)} all-to-all(bf16[32,72,128]{2,1,0:T(8,128)(2,1)S(1)} %shard_map.68), channel_id=1, replica_groups=mesh['dp'=32,'fsdp'=32] {'dp'}, dimensions={0} | all-to-all | bytes 1179648 | tf_op jit(solution)/shard_map/all_to_all | solution.py:244
  31.6 0.0 copy-done
  31.6 0.0 copy-done.2
  31.6 0.0 copy-done.1
  31.6 1.1 shard_map.70
  32.7 1.9 %collective-permute-start = (f32[4,128,128]{2,1,0:T(8,128)S(1)}, f32[4,128,128]{2,1,0:T(8,128)S(1)}, u32[]{:S(2)}, u32[]{:S(2)}) collective-permute-start(f32[4,128,128]{2,1,0:T(8,128)S(1)} %shard_map.70), channel_id=1, source_target_pairs={{0,1},{1,0},{2,3},{3,2},{4,5},{5,4},{6,7},{7,6},{8,9},{9,8},{10,11... | collective-permute-start | bytes 786440 | tf_op jit(solution)/shard_map/ppermute | solution.py:234
  34.6 1.1 shard_map.69.keep_ref
  35.7 0.4 collective-permute-done.other_ref
  36.1 0.2 shard_map.71
  36.4 12.8 %all_to_all.26 = f16[4,136,128]{2,1,0:T(8,128)(2,1)S(1)} all-to-all(f16[4,136,128]{2,1,0:T(8,128)(2,1)S(1)} %convert_element_type.12), channel_id=1, replica_groups={{0,2,4,6},{1,3,5,7},{8,10,12,14},{9,11,13,15},{16,18,20,22},{17,19,21,2..., dimensions={0} | all-to-all | bytes 278528 | tf_op jit(solution)/shard_map/all_to_all | solution.py:232
  49.2 0.2 shard_map.72
  49.4 30.7 %all_to_all.27 = f16[4,136,128]{2,1,0:T(8,128)(2,1)S(1)} all-to-all(f16[4,136,128]{2,1,0:T(8,128)(2,1)S(1)} %convert_element_type.14), channel_id=1, replica_groups={{0,8,16,24},{1,9,17,25},{2,10,18,26},{3,11,19,27},{4,12,20,28},{5,13,21..., dimensions={0} | all-to-all | bytes 278528 | tf_op jit(solution)/shard_map/all_to_all | solution.py:233
  80.1 8.8 %all_to_all.28.in_ref = bf16[4,128,128]{2,1,0:T(8,128)(2,1)S(1)} all-to-all(bf16[4,128,128]{2,1,0:T(8,128)(2,1)S(1)} %shard_map.73), channel_id=1, replica_groups={{0,2,4,6},{1,3,5,7},{8,10,12,14},{9,11,13,15},{16,18,20,22},{17,19,21,2..., dimensions={0} | all-to-all | bytes 262144 | tf_op jit(solution)/shard_map/all_to_all | solution.py:232
  89.0 1.9 %collective-permute-start.1 = (bf16[4,128,128]{2,1,0:T(8,128)(2,1)S(1)}, bf16[4,128,128]{2,1,0:T(8,128)(2,1)S(1)}, u32[]{:S(2)}, u32[]{:S(2)}) collective-permute-start(bf16[4,128,128]{2,1,0:T(8,128)(2,1)S(1)} %all_to_all.28.in_ref), channel_id=1, source_target_pairs={{0,1},{1,0},{2,3},{3,2},{4,5},{5,4},{6,7},{7,6},{8,9},{9,8},{10,11... | collective-permute-start | bytes 393224 | tf_op jit(solution)/shard_map/ppermute | solution.py:234
  90.9 1.1 shard_map.74.sum_ref
  92.0 0.2 collective-permute-done.1.in_ref
  92.2 1.2 shard_map.75
  93.4 24.1 %all_to_all.29.in_ref = bf16[32,72,128]{2,1,0:T(8,128)(2,1)S(1)} all-to-all(bf16[32,72,128]{2,1,0:T(8,128)(2,1)S(1)} %shard_map.75), channel_id=1, replica_groups=mesh['dp'=32,'fsdp'=32] {'dp'}, dimensions={0} | all-to-all | bytes 1179648 | tf_op jit(solution)/shard_map/all_to_all | solution.py:263
  117.4 0.7 shard_map.76
  (5 shorter events, 0.1 us)
Async XLA Ops:
  0.6 31.0 %copy-start = (bf16[4096,256]{1,0:T(8,128)(2,1)S(1)}, bf16[4096,256]{1,0:T(8,128)(2,1)}, u32[]{:S(2)}) copy-start(bf16[4096,256]{1,0:T(8,128)(2,1)} %act_ref.7) | copy-start | bytes 6291460
  0.6 31.0 %copy-start.2 = (s32[32,1]{0,1:T(1,128)S(1)}, s32[32,1]{0,1:T(1,128)}, u32[]{:S(2)}) copy-start(s32[32,1]{0,1:T(1,128)} %param.7) | copy-start | bytes 388
  0.7 0.9 copy-start.3
  1.5 0.7 copy-start.4
  2.2 29.4 %copy-start.1 = (bf16[4096,32]{0,1:T(8,128)(2,1)S(1)}, bf16[4096,32]{0,1:T(8,128)(2,1)}, u32[]{:S(2)}) copy-start(bf16[4096,32]{0,1:T(8,128)(2,1)} %param.6) | copy-start | bytes 786436
  32.7 3.4 %collective-permute-start = (f32[4,128,128]{2,1,0:T(8,128)S(1)}, f32[4,128,128]{2,1,0:T(8,128)S(1)}, u32[]{:S(2)}, u32[]{:S(2)}) collective-permute-start(f32[4,128,128]{2,1,0:T(8,128)S(1)} %shard_map.70), channel_id=1, source_target_pairs={{0,1},{1,0},{2,3},{3,2},{4,5},{5,4},{6,7},{7,6},{8,9},{9,8},{10,11... | collective-permute-start | bytes 786440 | tf_op jit(solution)/shard_map/ppermute | solution.py:234
  89.0 3.2 %collective-permute-start.1 = (bf16[4,128,128]{2,1,0:T(8,128)(2,1)S(1)}, bf16[4,128,128]{2,1,0:T(8,128)(2,1)S(1)}, u32[]{:S(2)}, u32[]{:S(2)}) collective-permute-start(bf16[4,128,128]{2,1,0:T(8,128)(2,1)S(1)} %all_to_all.28.in_ref), channel_id=1, source_target_pairs={{0,1},{1,0},{2,3},{3,2},{4,5},{5,4},{6,7},{7,6},{8,9},{9,8},{10,11... | collective-permute-start | bytes 393224 | tf_op jit(solution)/shard_map/ppermute | solution.py:234

commit v4 on v3

--- a/solution.py
+++ b/solution.py
@@ -23,7 +23,6 @@
 NT = (((1,), (1,)), ((), ()))
 NN = (((1,), (0,)), ((), ()))
 VMEM = pl.BlockSpec(memory_space=pltpu.VMEM)
-SMEM = pl.BlockSpec(memory_space=pltpu.SMEM)
 MIB = 1024 * 1024
 AHEAD = pl.CostEstimate(flops=10_000_000_000, bytes_accessed=20_000_000, transcendentals=0)
 HALF = pl.CostEstimate(flops=2_000_000_000, bytes_accessed=4_000_000, transcendentals=0)
@@ -45,17 +44,17 @@
     return lax.broadcasted_iota(jnp.int32, (8, 128), 1) // 32
 
 
-def pack_kernel(a_ref, b_ref, out_ref):
+def pack_kernel(ab_ref, out_ref):
     pieces = []
     for i in range(2):
-        pieces += [a_ref[i, :, 0:128], a_ref[i, :, 128:256]]
+        pieces += [ab_ref[i, :, 0:128], ab_ref[i, :, 128:256]]
     rows = lax.broadcasted_iota(jnp.int32, (32, 128), 0)
     lanes = lax.broadcasted_iota(jnp.int32, (32, 128), 1)
     small = jnp.zeros((8, 128), F32)
     for i in range(2):
         for h in range(2):
             place = jnp.where(lanes == rows + 32 * (2 * i + h), 1.0, 0.0).astype(BF16)
-            spread = lax.dot_general(b_ref[i], place, NN, preferred_element_type=F32)
+            spread = lax.dot_general(ab_ref[i, :, 256:288], place, NN, preferred_element_type=F32)
             small = small + spread[8 * h : 8 * h + 8]
     big = jnp.concatenate(pieces, axis=0)
     small = small.astype(BF16)
@@ -68,6 +67,11 @@
     return 2 * NEAR * a + 2 * b + parity
 
 
+def domains_of(ids_ref, parity):
+    ids = ids_ref[...]
+    return [jnp.where(parity == 1, ids[0, 2 * n + 1], ids[0, 2 * n]) for n in range(SHARE)]
+
+
 def tile_og(og_ref, tile):
     og = og_ref[:, pl.ds(pl.multiple_of(tile * TILE, TILE), TILE)]
     return jnp.concatenate([og, og, og, og], axis=0)
@@ -101,11 +105,12 @@
 
 def partial_kernel(own, ids_ref, w_ref, act_ref, og_ref, out_ref):
     parity = parity_of(own)
+    domains = domains_of(ids_ref, parity)
     block = lane_block()
     for b in range(NEAR):
         for a in range(FAR):
             tile = tile_at(b, a, parity)
-            e = ids_ref[tile]
+            e = domains[NEAR * a + b]
             o = e // 2
             i = e % 2
             w = w_ref[o, pl.ds(pl.multiple_of(i * 32, 32), 32), :]
@@ -180,6 +185,7 @@
 
 def add_grads(own, ids_ref, act_ref, og_ref, in_ref, acc_ref, ga_ref, gb_ref):
     parity = parity_of(own)
+    domains = domains_of(ids_ref, parity)
     block = lane_block()
     places = [(b, a) for b in range(NEAR) for a in range(FAR)]
     for n, (b, a) in enumerate(places):
@@ -189,7 +195,7 @@
         ga_ref[n] = lax.dot_general(up, tile_act(act_ref, tile), NN, preferred_element_type=F32)
         gb_ref[n] = lax.dot_general(down, tile_og(og_ref, tile), NT, preferred_element_type=F32)
     for n, (b, a) in enumerate(places):
-        e = ids_ref[tile_at(b, a, parity)]
+        e = domains[NEAR * a + b]
         o = e // 2
         i = e % 2
         ga = ga_ref[n]
@@ -224,7 +230,7 @@
 
 def shards(activations, out_grads, tile_domain, adapter_a, adapter_b):
     shape = jax.ShapeDtypeStruct
-    ids = tile_domain[:, 0]
+    ids = tile_domain.reshape(1, tile_domain.shape[0])
     og = out_grads.T
     pair = [(f, f ^ 1) for f in range(2 * SHARE)]
     near_groups = [[2 * (NEAR * a + b) + c for b in range(NEAR)] for a in range(FAR) for c in range(2)]
@@ -236,15 +242,14 @@
     packed = call(
         pack_kernel,
         shape((OWNERS, ROWS, 128), BF16),
-        [VMEM, VMEM],
-        adapter_a,
-        adapter_b,
+        [VMEM],
+        jnp.concatenate([adapter_a, adapter_b], axis=2),
         cost=AHEAD,
     )
     weights = lax.all_to_all(packed, "dp", 0, 0, tiled=True)
     inputs = (ids, weights, activations, og)
     part = shape((NEAR, FAR * 32, 128), F32)
-    kinds = [SMEM, VMEM, VMEM, VMEM]
+    kinds = [VMEM, VMEM, VMEM, VMEM]
     send = call(functools.partial(partial_kernel, False), part, kinds, *inputs, cost=HALF)
     keep = call(functools.partial(partial_kernel, True), part, kinds, *inputs, cost=HALF)
     scaled = shape((NEAR, SENT, 128), F32)

time: 119 us -> 117 us (0.983)
  the two profiles are of different devices: /device:TPU:2 before, /device:TPU:8 now
where the time goes in v4:
time: 117 us
  blocking collectives  106 us (91%)
  starting transfers between devices  3.84 us (3%)
  Pallas kernels  3.82 us (3%)
  waiting for transfers between devices  1.6 us (1%)
    all_to_all x1, blocking collectives, shards(): lax.all_to_all(x, 'fsdp', 0, 0, tiled=True, axis_index_groups=far_groups)  30.7 us
    all_to_all x1, blocking collectives, shards(): weights = lax.all_to_all(packed, 'dp', 0, 0, tiled=True)  29.7 us
    all_to_all x1, blocking collectives, shards(): summed = lax.all_to_all(grads, 'dp', 0, 0, tiled=True)  23.9 us
    all_to_all x2, blocking collectives, shards(): lax.all_to_all(x, 'fsdp', 0, 0, tiled=True, axis_index_groups=near_groups)  21.5 us
    ppermute x2, starting transfers between devices, shards(): swap = lambda x: lax.ppermute(x, 'fsdp', pair)  3.84 us
    pallas_call x9, Pallas kernels, call(): pl.pallas_call(kernel, out_shape=out, in_specs=specs, out_specs=jax.tree....  3.82 us
  transfers between devices with their start and end apart: 2, of which 2 were waited for; matrix products, arithmetic and copies ran while one was open for 0% of the time, Pallas kernels for 1%

profile of v4, /device:TPU:8, one launch (start us, length us, event | category | flops | bytes accessed | tf_op | source)
XLA Modules:
  0.0 116.6 jit_solution(9626381961640073159)
XLA Ops:
  0.6 0.7 pad_maximum_fusion.ab_ref
  1.4 0.0 copy-start
  1.4 0.0 copy-start.1
  1.4 0.0 copy-start.2
  1.4 0.2 shard_map.68
  1.6 29.7 %all_to_all.25.w_ref = bf16[32,72,128]{2,1,0:T(8,128)(2,1)S(1)} all-to-all(bf16[32,72,128]{2,1,0:T(8,128)(2,1)S(1)} %shard_map.68), channel_id=1, replica_groups=mesh['dp'=32,'fsdp'=32] {'dp'}, dimensions={0} | all-to-all | bytes 1179648 | tf_op jit(solution)/shard_map/all_to_all | solution.py:249
  31.2 0.0 copy-done
  31.3 0.0 copy-done.1
  31.3 0.0 copy-done.2
  31.3 0.6 shard_map.70
  31.9 1.9 %collective-permute-start = (f32[4,128,128]{2,1,0:T(8,128)S(1)}, f32[4,128,128]{2,1,0:T(8,128)S(1)}, u32[]{:S(2)}, u32[]{:S(2)}) collective-permute-start(f32[4,128,128]{2,1,0:T(8,128)S(1)} %shard_map.70), channel_id=1, source_target_pairs={{0,1},{1,0},{2,3},{3,2},{4,5},{5,4},{6,7},{7,6},{8,9},{9,8},{10,11... | collective-permute-start | bytes 786440 | tf_op jit(solution)/shard_map/ppermute | solution.py:240
  33.8 0.6 shard_map.69.keep_ref
  34.5 0.9 collective-permute-done.other_ref
  35.3 0.2 shard_map.71
  35.6 12.7 %all_to_all.26 = f16[4,136,128]{2,1,0:T(8,128)(2,1)S(1)} all-to-all(f16[4,136,128]{2,1,0:T(8,128)(2,1)S(1)} %convert_element_type.12), channel_id=1, replica_groups={{0,2,4,6},{1,3,5,7},{8,10,12,14},{9,11,13,15},{16,18,20,22},{17,19,21,2..., dimensions={0} | all-to-all | bytes 278528 | tf_op jit(solution)/shard_map/all_to_all | solution.py:238
  48.3 0.2 shard_map.72
  48.5 30.7 %all_to_all.27 = f16[4,136,128]{2,1,0:T(8,128)(2,1)S(1)} all-to-all(f16[4,136,128]{2,1,0:T(8,128)(2,1)S(1)} %convert_element_type.14), channel_id=1, replica_groups={{0,8,16,24},{1,9,17,25},{2,10,18,26},{3,11,19,27},{4,12,20,28},{5,13,21..., dimensions={0} | all-to-all | bytes 278528 | tf_op jit(solution)/shard_map/all_to_all | solution.py:239
  79.2 8.8 %all_to_all.28.in_ref = bf16[4,128,128]{2,1,0:T(8,128)(2,1)S(1)} all-to-all(bf16[4,128,128]{2,1,0:T(8,128)(2,1)S(1)} %shard_map.73), channel_id=1, replica_groups={{0,2,4,6},{1,3,5,7},{8,10,12,14},{9,11,13,15},{16,18,20,22},{17,19,21,2..., dimensions={0} | all-to-all | bytes 262144 | tf_op jit(solution)/shard_map/all_to_all | solution.py:238
  88.1 1.9 %collective-permute-start.1 = (bf16[4,128,128]{2,1,0:T(8,128)(2,1)S(1)}, bf16[4,128,128]{2,1,0:T(8,128)(2,1)S(1)}, u32[]{:S(2)}, u32[]{:S(2)}) collective-permute-start(bf16[4,128,128]{2,1,0:T(8,128)(2,1)S(1)} %all_to_all.28.in_ref), channel_id=1, source_target_pairs={{0,1},{1,0},{2,3},{3,2},{4,5},{5,4},{6,7},{7,6},{8,9},{9,8},{10,11... | collective-permute-start | bytes 393224 | tf_op jit(solution)/shard_map/ppermute | solution.py:240
  90.0 0.6 shard_map.74.sum_ref
  90.5 0.7 collective-permute-done.1.in_ref
  91.3 0.7 shard_map.75
  91.9 23.9 %all_to_all.29.in_ref = bf16[32,72,128]{2,1,0:T(8,128)(2,1)S(1)} all-to-all(bf16[32,72,128]{2,1,0:T(8,128)(2,1)S(1)} %shard_map.75), channel_id=1, replica_groups=mesh['dp'=32,'fsdp'=32] {'dp'}, dimensions={0} | all-to-all | bytes 1179648 | tf_op jit(solution)/shard_map/all_to_all | solution.py:268
  115.9 0.7 shard_map.76
  (5 shorter events, 0.1 us)
Async XLA Ops:
  1.4 29.9 %copy-start = (bf16[4096,256]{1,0:T(8,128)(2,1)S(1)}, bf16[4096,256]{1,0:T(8,128)(2,1)}, u32[]{:S(2)}) copy-start(bf16[4096,256]{1,0:T(8,128)(2,1)} %act_ref.7) | copy-start | bytes 6291460
  1.4 29.9 %copy-start.1 = (bf16[4096,32]{0,1:T(8,128)(2,1)S(1)}, bf16[4096,32]{0,1:T(8,128)(2,1)}, u32[]{:S(2)}) copy-start(bf16[4096,32]{0,1:T(8,128)(2,1)} %param.6) | copy-start | bytes 786436
  1.4 29.9 %copy-start.2 = (s32[32,1]{0,1:T(1,128)S(1)}, s32[32,1]{0,1:T(1,128)}, u32[]{:S(2)}) copy-start(s32[32,1]{0,1:T(1,128)} %param.7) | copy-start | bytes 388
  31.9 3.4 %collective-permute-start = (f32[4,128,128]{2,1,0:T(8,128)S(1)}, f32[4,128,128]{2,1,0:T(8,128)S(1)}, u32[]{:S(2)}, u32[]{:S(2)}) collective-permute-start(f32[4,128,128]{2,1,0:T(8,128)S(1)} %shard_map.70), channel_id=1, source_target_pairs={{0,1},{1,0},{2,3},{3,2},{4,5},{5,4},{6,7},{7,6},{8,9},{9,8},{10,11... | collective-permute-start | bytes 786440 | tf_op jit(solution)/shard_map/ppermute | solution.py:240
  88.1 3.2 %collective-permute-start.1 = (bf16[4,128,128]{2,1,0:T(8,128)(2,1)S(1)}, bf16[4,128,128]{2,1,0:T(8,128)(2,1)S(1)}, u32[]{:S(2)}, u32[]{:S(2)}) collective-permute-start(bf16[4,128,128]{2,1,0:T(8,128)(2,1)S(1)} %all_to_all.28.in_ref), channel_id=1, source_target_pairs={{0,1},{1,0},{2,3},{3,2},{4,5},{5,4},{6,7},{7,6},{8,9},{9,8},{10,11... | collective-permute-start | bytes 393224 | tf_op jit(solution)/shard_map/ppermute | solution.py:240

commit v5 on v4

--- a/solution.py
+++ b/solution.py
@@ -155,20 +155,23 @@
 
 
 def near_kernel(in_ref, out_ref):
-    downs, ups = summed_parts(in_ref, NEAR)
-    down_top, up_top = jnp.abs(downs[0]), jnp.abs(ups[0])
-    for a in range(1, FAR):
-        down_top = jnp.maximum(down_top, jnp.abs(downs[a]))
-        up_top = jnp.maximum(up_top, jnp.abs(ups[a]))
-    root = scale_of(down_top, up_top)
-    factor = TOP / fourth(root)
-    down_factor, up_factor = widen(factor[0:1]), widen(factor[1:2])
+    sizes = [fourth(in_ref[q, FAR * 32 : SENT]) for q in range(NEAR)]
+    root = jnp.sqrt(jnp.sqrt(sum(sizes[1:], sizes[0]))).astype(BF16).astype(F32)
+    share = 1.0 / fourth(root)
+    factors = []
+    for size in sizes:
+        factor = size * share
+        factors.append((widen(factor[0:1]), widen(factor[1:2])))
     for a in range(FAR):
-        down = downs[a] * down_factor
-        up = ups[a] * up_factor
+        at, to = 32 * a, 32 * a + 16
+        down = in_ref[0, at:to] * factors[0][0]
+        up = in_ref[0, to : to + 16] * factors[0][1]
+        for q in range(1, NEAR):
+            down = down + in_ref[q, at:to] * factors[q][0]
+            up = up + in_ref[q, to : to + 16] * factors[q][1]
         for f in range(FAR):
-            out_ref[f, 32 * a : 32 * a + 16] = down
-            out_ref[f, 32 * a + 16 : 32 * a + 32] = up
+            out_ref[f, at:to] = down
+            out_ref[f, to : to + 16] = up
     for f in range(FAR):
         out_ref[f, FAR * 32 : SENT] = root
 

time: 117 us -> 117 us (level)
  no operation moved by 1% of the time
where the time goes in v5:
time: 117 us; the launch traced here: 116 us
  blocking collectives  106 us (91%)
  starting transfers between devices  3.84 us (3%)
  Pallas kernels  3.69 us (3%)
  waiting for transfers between devices  1.61 us (1%)
    all_to_all x1, blocking collectives, shards(): lax.all_to_all(x, 'fsdp', 0, 0, tiled=True, axis_index_groups=far_groups)  30.7 us
    all_to_all x1, blocking collectives, shards(): weights = lax.all_to_all(packed, 'dp', 0, 0, tiled=True)  29.7 us
    all_to_all x1, blocking collectives, shards(): summed = lax.all_to_all(grads, 'dp', 0, 0, tiled=True)  23.9 us
    all_to_all x2, blocking collectives, shards(): lax.all_to_all(x, 'fsdp', 0, 0, tiled=True, axis_index_groups=near_groups)  21.5 us
    ppermute x2, starting transfers between devices, shards(): swap = lambda x: lax.ppermute(x, 'fsdp', pair)  3.84 us
    pallas_call x9, Pallas kernels, call(): pl.pallas_call(kernel, out_shape=out, in_specs=specs, out_specs=jax.tree....  3.69 us
  transfers between devices with their start and end apart: 2, of which 2 were waited for; matrix products, arithmetic and copies ran while one was open for 0% of the time, Pallas kernels for 1%

profile of v5, /device:TPU:8, one launch (start us, length us, event | category | flops | bytes accessed | tf_op | source)
XLA Modules:
  0.0 116.4 jit_solution(4052555198755033402)
XLA Ops:
  0.6 0.7 pad_maximum_fusion.ab_ref
  1.4 0.0 copy-start
  1.4 0.0 copy-start.1
  1.4 0.0 copy-start.2
  1.4 0.2 shard_map.68
  1.6 29.7 %all_to_all.25.w_ref = bf16[32,72,128]{2,1,0:T(8,128)(2,1)S(1)} all-to-all(bf16[32,72,128]{2,1,0:T(8,128)(2,1)S(1)} %shard_map.68), channel_id=1, replica_groups=mesh['dp'=32,'fsdp'=32] {'dp'}, dimensions={0} | all-to-all | bytes 1179648 | tf_op jit(solution)/shard_map/all_to_all | solution.py:252
  31.2 0.0 copy-done
  31.3 0.0 copy-done.1
  31.3 0.0 copy-done.2
  31.3 0.6 shard_map.70
  31.9 1.9 %collective-permute-start = (f32[4,128,128]{2,1,0:T(8,128)S(1)}, f32[4,128,128]{2,1,0:T(8,128)S(1)}, u32[]{:S(2)}, u32[]{:S(2)}) collective-permute-start(f32[4,128,128]{2,1,0:T(8,128)S(1)} %shard_map.70), channel_id=1, source_target_pairs={{0,1},{1,0},{2,3},{3,2},{4,5},{5,4},{6,7},{7,6},{8,9},{9,8},{10,11... | collective-permute-start | bytes 786440 | tf_op jit(solution)/shard_map/ppermute | solution.py:243
  33.8 0.6 shard_map.69.keep_ref
  34.5 0.9 collective-permute-done.other_ref
  35.3 0.2 shard_map.71
  35.6 12.7 %all_to_all.26 = f16[4,136,128]{2,1,0:T(8,128)(2,1)S(1)} all-to-all(f16[4,136,128]{2,1,0:T(8,128)(2,1)S(1)} %convert_element_type.12), channel_id=1, replica_groups={{0,2,4,6},{1,3,5,7},{8,10,12,14},{9,11,13,15},{16,18,20,22},{17,19,21,2..., dimensions={0} | all-to-all | bytes 278528 | tf_op jit(solution)/shard_map/all_to_all | solution.py:241
  48.3 0.1 shard_map.72
  48.4 30.7 %all_to_all.27 = f16[4,136,128]{2,1,0:T(8,128)(2,1)S(1)} all-to-all(f16[4,136,128]{2,1,0:T(8,128)(2,1)S(1)} %convert_element_type.14), channel_id=1, replica_groups={{0,8,16,24},{1,9,17,25},{2,10,18,26},{3,11,19,27},{4,12,20,28},{5,13,21..., dimensions={0} | all-to-all | bytes 278528 | tf_op jit(solution)/shard_map/all_to_all | solution.py:242
  79.1 8.8 %all_to_all.28.in_ref = bf16[4,128,128]{2,1,0:T(8,128)(2,1)S(1)} all-to-all(bf16[4,128,128]{2,1,0:T(8,128)(2,1)S(1)} %shard_map.73), channel_id=1, replica_groups={{0,2,4,6},{1,3,5,7},{8,10,12,14},{9,11,13,15},{16,18,20,22},{17,19,21,2..., dimensions={0} | all-to-all | bytes 262144 | tf_op jit(solution)/shard_map/all_to_all | solution.py:241
  87.9 1.9 %collective-permute-start.1 = (bf16[4,128,128]{2,1,0:T(8,128)(2,1)S(1)}, bf16[4,128,128]{2,1,0:T(8,128)(2,1)S(1)}, u32[]{:S(2)}, u32[]{:S(2)}) collective-permute-start(bf16[4,128,128]{2,1,0:T(8,128)(2,1)S(1)} %all_to_all.28.in_ref), channel_id=1, source_target_pairs={{0,1},{1,0},{2,3},{3,2},{4,5},{5,4},{6,7},{7,6},{8,9},{9,8},{10,11... | collective-permute-start | bytes 393224 | tf_op jit(solution)/shard_map/ppermute | solution.py:243
  89.8 0.6 shard_map.74.sum_ref
  90.4 0.7 collective-permute-done.1.in_ref
  91.2 0.7 shard_map.75
  91.8 23.9 %all_to_all.29.in_ref = bf16[32,72,128]{2,1,0:T(8,128)(2,1)S(1)} all-to-all(bf16[32,72,128]{2,1,0:T(8,128)(2,1)S(1)} %shard_map.75), channel_id=1, replica_groups=mesh['dp'=32,'fsdp'=32] {'dp'}, dimensions={0} | all-to-all | bytes 1179648 | tf_op jit(solution)/shard_map/all_to_all | solution.py:271
  115.7 0.7 shard_map.76
  (5 shorter events, 0.1 us)
Async XLA Ops:
  1.4 29.9 %copy-start = (bf16[4096,256]{1,0:T(8,128)(2,1)S(1)}, bf16[4096,256]{1,0:T(8,128)(2,1)}, u32[]{:S(2)}) copy-start(bf16[4096,256]{1,0:T(8,128)(2,1)} %act_ref.7) | copy-start | bytes 6291460
  1.4 29.9 %copy-start.1 = (bf16[4096,32]{0,1:T(8,128)(2,1)S(1)}, bf16[4096,32]{0,1:T(8,128)(2,1)}, u32[]{:S(2)}) copy-start(bf16[4096,32]{0,1:T(8,128)(2,1)} %param.6) | copy-start | bytes 786436
  1.4 29.9 %copy-start.2 = (s32[32,1]{0,1:T(1,128)S(1)}, s32[32,1]{0,1:T(1,128)}, u32[]{:S(2)}) copy-start(s32[32,1]{0,1:T(1,128)} %param.7) | copy-start | bytes 388
  31.9 3.4 %collective-permute-start = (f32[4,128,128]{2,1,0:T(8,128)S(1)}, f32[4,128,128]{2,1,0:T(8,128)S(1)}, u32[]{:S(2)}, u32[]{:S(2)}) collective-permute-start(f32[4,128,128]{2,1,0:T(8,128)S(1)} %shard_map.70), channel_id=1, source_target_pairs={{0,1},{1,0},{2,3},{3,2},{4,5},{5,4},{6,7},{7,6},{8,9},{9,8},{10,11... | collective-permute-start | bytes 786440 | tf_op jit(solution)/shard_map/ppermute | solution.py:243
  87.9 3.2 %collective-permute-start.1 = (bf16[4,128,128]{2,1,0:T(8,128)(2,1)S(1)}, bf16[4,128,128]{2,1,0:T(8,128)(2,1)S(1)}, u32[]{:S(2)}, u32[]{:S(2)}) collective-permute-start(bf16[4,128,128]{2,1,0:T(8,128)(2,1)S(1)} %all_to_all.28.in_ref), channel_id=1, source_target_pairs={{0,1},{1,0},{2,3},{3,2},{4,5},{5,4},{6,7},{7,6},{8,9},{9,8},{10,11... | collective-permute-start | bytes 393224 | tf_op jit(solution)/shard_map/ppermute | solution.py:243

commit v6 on v4

--- a/solution.py
+++ b/solution.py
@@ -125,12 +125,11 @@
             out_ref[b, 32 * a + 16 : 32 * a + 32] = up
 
 
-def chip_kernel(keep_ref, other_ref, out_ref, part_ref):
+def chip_kernel(keep_ref, other_ref, out_ref):
     down_top = jnp.zeros((RANK, TILE), F32)
     up_top = jnp.zeros((RANK, TILE), F32)
     for b in range(NEAR):
         part = keep_ref[b] + other_ref[b]
-        part_ref[b] = part
         for a in range(FAR):
             down_top = jnp.maximum(down_top, jnp.abs(part[32 * a : 32 * a + 16]))
             up_top = jnp.maximum(up_top, jnp.abs(part[32 * a + 16 : 32 * a + 32]))
@@ -138,7 +137,7 @@
     factor = TOP / fourth(root)
     both = jnp.concatenate([widen(factor[0:1]), widen(factor[1:2])] * FAR, axis=0)
     for b in range(NEAR):
-        out_ref[b, 0 : FAR * 32] = part_ref[b] * both
+        out_ref[b, 0 : FAR * 32] = (keep_ref[b] + other_ref[b]) * both
         out_ref[b, FAR * 32 : SENT] = root
 
 
@@ -253,7 +252,7 @@
     send = call(functools.partial(partial_kernel, False), part, kinds, *inputs, cost=HALF)
     keep = call(functools.partial(partial_kernel, True), part, kinds, *inputs, cost=HALF)
     scaled = shape((NEAR, SENT, 128), F32)
-    chip = call(chip_kernel, scaled, [VMEM, VMEM], keep, swap(send), scratch=[pltpu.VMEM(part.shape, F32)])
+    chip = call(chip_kernel, scaled, [VMEM, VMEM], keep, swap(send))
     chip = near(chip.astype(F16)).astype(F32)
     part = call(near_kernel, shape((FAR, SENT, 128), F32), [VMEM], chip)
     part = far(part.astype(F16)).astype(F32)

time: 117 us -> 117 us (level)
  no operation moved by 1% of the time
where the time goes in v6:
time: 117 us
  blocking collectives  106 us (91%)
  starting transfers between devices  3.84 us (3%)
  Pallas kernels  3.82 us (3%)
  waiting for transfers between devices  1.61 us (1%)
    all_to_all x1, blocking collectives, shards(): lax.all_to_all(x, 'fsdp', 0, 0, tiled=True, axis_index_groups=far_groups)  30.7 us
    all_to_all x1, blocking collectives, shards(): weights = lax.all_to_all(packed, 'dp', 0, 0, tiled=True)  29.7 us
    all_to_all x1, blocking collectives, shards(): summed = lax.all_to_all(grads, 'dp', 0, 0, tiled=True)  23.9 us
    all_to_all x2, blocking collectives, shards(): lax.all_to_all(x, 'fsdp', 0, 0, tiled=True, axis_index_groups=near_groups)  21.5 us
    ppermute x2, starting transfers between devices, shards(): swap = lambda x: lax.ppermute(x, 'fsdp', pair)  3.84 us
    pallas_call x9, Pallas kernels, call(): pl.pallas_call(kernel, out_shape=out, in_specs=specs, out_specs=jax.tree....  3.82 us
  transfers between devices with their start and end apart: 2, of which 2 were waited for; matrix products, arithmetic and copies ran while one was open for 0% of the time, Pallas kernels for 1%

profile of v6, /device:TPU:8, one launch (start us, length us, event | category | flops | bytes accessed | tf_op | source)
XLA Modules:
  0.0 116.6 jit_solution(9626381961640073159)
XLA Ops:
  0.6 0.7 pad_maximum_fusion.ab_ref
  1.4 0.0 copy-start
  1.4 0.0 copy-start.1
  1.4 0.0 copy-start.2
  1.4 0.2 shard_map.68
  1.6 29.7 %all_to_all.25.w_ref = bf16[32,72,128]{2,1,0:T(8,128)(2,1)S(1)} all-to-all(bf16[32,72,128]{2,1,0:T(8,128)(2,1)S(1)} %shard_map.68), channel_id=1, replica_groups=mesh['dp'=32,'fsdp'=32] {'dp'}, dimensions={0} | all-to-all | bytes 1179648 | tf_op jit(solution)/shard_map/all_to_all | solution.py:248
  31.2 0.0 copy-done
  31.3 0.0 copy-done.1
  31.3 0.0 copy-done.2
  31.3 0.6 shard_map.70
  31.9 1.9 %collective-permute-start = (f32[4,128,128]{2,1,0:T(8,128)S(1)}, f32[4,128,128]{2,1,0:T(8,128)S(1)}, u32[]{:S(2)}, u32[]{:S(2)}) collective-permute-start(f32[4,128,128]{2,1,0:T(8,128)S(1)} %shard_map.70), channel_id=1, source_target_pairs={{0,1},{1,0},{2,3},{3,2},{4,5},{5,4},{6,7},{7,6},{8,9},{9,8},{10,11... | collective-permute-start | bytes 786440 | tf_op jit(solution)/shard_map/ppermute | solution.py:239
  33.8 0.6 shard_map.69.keep_ref
  34.5 0.9 collective-permute-done.other_ref
  35.3 0.2 shard_map.71
  35.6 12.7 %all_to_all.26 = f16[4,136,128]{2,1,0:T(8,128)(2,1)S(1)} all-to-all(f16[4,136,128]{2,1,0:T(8,128)(2,1)S(1)} %convert_element_type.12), channel_id=1, replica_groups={{0,2,4,6},{1,3,5,7},{8,10,12,14},{9,11,13,15},{16,18,20,22},{17,19,21,2..., dimensions={0} | all-to-all | bytes 278528 | tf_op jit(solution)/shard_map/all_to_all | solution.py:237
  48.3 0.2 shard_map.72
  48.5 30.7 %all_to_all.27 = f16[4,136,128]{2,1,0:T(8,128)(2,1)S(1)} all-to-all(f16[4,136,128]{2,1,0:T(8,128)(2,1)S(1)} %convert_element_type.14), channel_id=1, replica_groups={{0,8,16,24},{1,9,17,25},{2,10,18,26},{3,11,19,27},{4,12,20,28},{5,13,21..., dimensions={0} | all-to-all | bytes 278528 | tf_op jit(solution)/shard_map/all_to_all | solution.py:238
  79.2 8.8 %all_to_all.28.in_ref = bf16[4,128,128]{2,1,0:T(8,128)(2,1)S(1)} all-to-all(bf16[4,128,128]{2,1,0:T(8,128)(2,1)S(1)} %shard_map.73), channel_id=1, replica_groups={{0,2,4,6},{1,3,5,7},{8,10,12,14},{9,11,13,15},{16,18,20,22},{17,19,21,2..., dimensions={0} | all-to-all | bytes 262144 | tf_op jit(solution)/shard_map/all_to_all | solution.py:237
  88.1 1.9 %collective-permute-start.1 = (bf16[4,128,128]{2,1,0:T(8,128)(2,1)S(1)}, bf16[4,128,128]{2,1,0:T(8,128)(2,1)S(1)}, u32[]{:S(2)}, u32[]{:S(2)}) collective-permute-start(bf16[4,128,128]{2,1,0:T(8,128)(2,1)S(1)} %all_to_all.28.in_ref), channel_id=1, source_target_pairs={{0,1},{1,0},{2,3},{3,2},{4,5},{5,4},{6,7},{7,6},{8,9},{9,8},{10,11... | collective-permute-start | bytes 393224 | tf_op jit(solution)/shard_map/ppermute | solution.py:239
  90.0 0.6 shard_map.74.sum_ref
  90.5 0.7 collective-permute-done.1.in_ref
  91.3 0.7 shard_map.75
  91.9 23.9 %all_to_all.29.in_ref = bf16[32,72,128]{2,1,0:T(8,128)(2,1)S(1)} all-to-all(bf16[32,72,128]{2,1,0:T(8,128)(2,1)S(1)} %shard_map.75), channel_id=1, replica_groups=mesh['dp'=32,'fsdp'=32] {'dp'}, dimensions={0} | all-to-all | bytes 1179648 | tf_op jit(solution)/shard_map/all_to_all | solution.py:267
  115.9 0.7 shard_map.76
  (5 shorter events, 0.1 us)
Async XLA Ops:
  1.4 29.9 %copy-start = (bf16[4096,256]{1,0:T(8,128)(2,1)S(1)}, bf16[4096,256]{1,0:T(8,128)(2,1)}, u32[]{:S(2)}) copy-start(bf16[4096,256]{1,0:T(8,128)(2,1)} %act_ref.7) | copy-start | bytes 6291460
  1.4 29.9 %copy-start.1 = (bf16[4096,32]{0,1:T(8,128)(2,1)S(1)}, bf16[4096,32]{0,1:T(8,128)(2,1)}, u32[]{:S(2)}) copy-start(bf16[4096,32]{0,1:T(8,128)(2,1)} %param.6) | copy-start | bytes 786436
  1.4 29.9 %copy-start.2 = (s32[32,1]{0,1:T(1,128)S(1)}, s32[32,1]{0,1:T(1,128)}, u32[]{:S(2)}) copy-start(s32[32,1]{0,1:T(1,128)} %param.7) | copy-start | bytes 388
  31.9 3.4 %collective-permute-start = (f32[4,128,128]{2,1,0:T(8,128)S(1)}, f32[4,128,128]{2,1,0:T(8,128)S(1)}, u32[]{:S(2)}, u32[]{:S(2)}) collective-permute-start(f32[4,128,128]{2,1,0:T(8,128)S(1)} %shard_map.70), channel_id=1, source_target_pairs={{0,1},{1,0},{2,3},{3,2},{4,5},{5,4},{6,7},{7,6},{8,9},{9,8},{10,11... | collective-permute-start | bytes 786440 | tf_op jit(solution)/shard_map/ppermute | solution.py:239
  88.1 3.2 %collective-permute-start.1 = (bf16[4,128,128]{2,1,0:T(8,128)(2,1)S(1)}, bf16[4,128,128]{2,1,0:T(8,128)(2,1)S(1)}, u32[]{:S(2)}, u32[]{:S(2)}) collective-permute-start(bf16[4,128,128]{2,1,0:T(8,128)(2,1)S(1)} %all_to_all.28.in_ref), channel_id=1, source_target_pairs={{0,1},{1,0},{2,3},{3,2},{4,5},{5,4},{6,7},{7,6},{8,9},{9,8},{10,11... | collective-permute-start | bytes 393224 | tf_op jit(solution)/shard_map/ppermute | solution.py:239
